TPU v7x, 256 devices: a whole 4x4x8 slice. The times are simulated.
256 devices in a mesh: dp: 32 (over x, y, core), mp: 8 (over z).
Axes of the slice: x: 4, y: 4, z: 8, core: 2. Of those that a mesh axis runs over, the one named last changes fastest.
Arguments:
- grad_down: bfloat16 [32, 4096, 5120], P('dp', None, 'mp'), may hold values from -6 to 6
- grad_out: bfloat16 [32, 4096, 5120], P('dp', None, 'mp'), may hold values from -6 to 6
- momentum_down: float32 [4096, 5120], P('dp', 'mp'), as said below
- momentum_out: float32 [4096, 5120], P('dp', 'mp'), as said below
- master_down: float32 [4096, 5120], P('dp', 'mp'), may hold values from -6 to 6
- master_out: float32 [4096, 5120], P('dp', 'mp'), may hold values from -6 to 6
Outputs:
- new_momentum_down: float32 [4096, 5120], P('dp', 'mp')
- new_momentum_out: float32 [4096, 5120], P('dp', 'mp')
- weights_down: bfloat16 [4096, 5120], P(None, 'mp')
- weights_out: bfloat16 [4096, 5120], P(None, 'mp')
Inputs may be any that keep to these rules, and one draw needn't show every extreme that they name: `momentum_down`: real-valued momentum entries. `momentum_out`: real-valued momentum entries.
All inputs are finite; a program needn't handle non-finite values.
Results may differ from a plain program's by a relative error of at most 0.0004.
Values may be sent and summed in bfloat16 or wider, within the bound.
A program may use at most 128 MiB of HBM per device.

v0:
```python
import math

import jax
import jax.numpy as jnp
from jax import lax
from jax.sharding import PartitionSpec as P

D = 5120
ITERS = 3


momentum_coef = 0.95
learn_rate = 0.5
decay_rate = 0.1
coef_a = 3.4445
coef_b = -4.775
coef_c = 2.0315
norm_eps = 1e-07


def poly_step(x, gram):
    poly = coef_b * gram + coef_c * jnp.dot(
        gram, gram, precision=lax.Precision.HIGHEST, preferred_element_type=jnp.float32
    )
    return coef_a * x + jnp.dot(
        poly, x, precision=lax.Precision.HIGHEST, preferred_element_type=jnp.float32
    )


def self_gram(x):
    return jnp.dot(x, x.T, precision=lax.Precision.HIGHEST, preferred_element_type=jnp.float32)


def orthogonalize(blocks):
    sums = lax.psum(tuple((jnp.sum(b * b) for b in blocks)), "mp")
    states = [b / (jnp.sqrt(s) + norm_eps) for b, s in zip(blocks, sums)]
    for step in range(ITERS):
        grams = lax.psum(tuple((self_gram(x) for x in states)), "mp")
        states = [poly_step(x, g) for x, g in zip(states, grams)]
    return states


def finish(totals, momenta, masters):
    new_momenta = [momentum_coef * m + t for m, t in zip(momenta, totals)]
    looks = [t + momentum_coef * n for t, n in zip(totals, new_momenta)]
    orthos = orthogonalize(looks)
    factor = learn_rate * 0.2 * math.sqrt(D)
    weights = [
        ((1.0 - learn_rate * decay_rate) * w - factor * x).astype(jnp.bfloat16)
        for w, x in zip(masters, orthos)
    ]
    return (new_momenta, weights)


def body(grad_down, grad_out, momentum_down, momentum_out, master_down, master_out):
    totals = (
        lax.psum_scatter(grad_down[0].astype(jnp.float32), "dp", scatter_dimension=0, tiled=True),
        lax.psum_scatter(grad_out[0].astype(jnp.float32), "dp", scatter_dimension=0, tiled=True),
    )
    new_momenta, weights = finish(
        list(totals), [momentum_down, momentum_out], [master_down, master_out]
    )
    gathered = (
        lax.all_gather(weights[0], "dp", axis=0, tiled=True),
        lax.all_gather(weights[1], "dp", axis=0, tiled=True),
    )
    return (new_momenta[0], new_momenta[1], gathered[0], gathered[1])


def solution(mesh):
    placed = (
        P("dp", None, "mp"),
        P("dp", None, "mp"),
        P("dp", "mp"),
        P("dp", "mp"),
        P("dp", "mp"),
        P("dp", "mp"),
    )
    return jax.shard_map(
        body,
        mesh=mesh,
        in_specs=placed,
        out_specs=(P("dp", "mp"), P("dp", "mp"), P(None, "mp"), P(None, "mp")),
        check_vma=False,
    )
```

profile of v0, /device:TPU:1, one launch (start us, length us, event | category | flops | bytes accessed | tf_op | source)
XLA Modules:
  0.0 606.4 jit_solution(15270311908573478176)
XLA Ops:
  7.2 0.0 reduce-scatter.3.cloned.1.call-start
  7.2 7.1 %bitcast_convert_fusion.1 = f32[4096,640]{1,0:T(8,128)} fusion(bf16[1,4096,640]{2,1,0:T(8,128)(2,1)} %param.6), kind=kLoop, calls=%fused_computation.1 | loop fusion | flops 2621440 | bytes 15728640 | tf_op jit(solution)/shard_map/convert_element_type | solution.py:57
  14.4 0.0 reduce-scatter.3.cloned.1.call-update
  14.4 0.0 reduce-scatter.5.cloned.1.call-start
  14.4 7.0 %bitcast_convert_fusion = f32[4096,640]{1,0:T(8,128)} fusion(bf16[1,4096,640]{2,1,0:T(8,128)(2,1)} %param.7), kind=kLoop, calls=%fused_computation | loop fusion | flops 2621440 | bytes 15728640 | tf_op jit(solution)/shard_map/convert_element_type | solution.py:58
  21.4 0.0 copy-start.1
  21.4 0.0 copy-start.2
  21.4 0.0 reduce-scatter.5.cloned.1.call-update
  21.5 0.0 all-reduce.12.cloned.1.call-start
  21.5 101.5 %reduce-scatter.3.cloned.1.call-done = f32[128,640]{1,0:T(8,128)} async-done(((f32[4096,640]{1,0:T(8,128)}), f32[128,640]{1,0:T(8,128)}) %reduce-scatter.3.cloned.1.call-update) | async-done | bytes 327696 | tf_op jit(solution)/shard_map/reduce_scatter | solution.py:57
  123.0 0.0 copy-done.1
  123.0 1.7 multiply_reduce_fusion.1
  124.6 0.0 copy-start.5
  124.6 108.1 %reduce-scatter.5.cloned.1.call-done = f32[128,640]{1,0:T(8,128)} async-done(((f32[4096,640]{1,0:T(8,128)}), f32[128,640]{1,0:T(8,128)}) %reduce-scatter.5.cloned.1.call-update) | async-done | bytes 327696 | tf_op jit(solution)/shard_map/reduce_scatter | solution.py:58
  232.7 0.0 copy-done.2
  232.7 0.0 copy-start.7
  232.7 1.7 multiply_reduce_fusion
  234.4 0.0 copy-start.6
  234.4 14.3 %all-reduce = (f32[]{:T(128)}, f32[]{:T(128)}) all-reduce(f32[]{:T(128)} %get-tuple-element.14, f32[]{:T(128)} %get-tuple-element.12), channel_id=1, replica_groups=mesh['dp'=32,'mp'=8] {'mp'}, use_global_device_ids=true, to_apply=%region_3.0 | all-reduce | flops 2 | bytes 16 | tf_op jit(solution)/shard_map/psum | solution.py:35
  250.1 2.3 fusion.12
  252.4 2.3 fusion.13
  254.7 0.0 all-reduce.12.cloned.1.call-update
  254.7 0.0 all-reduce.10.cloned.1.call-start
  254.7 68.7 %all-reduce.12.cloned.1.call-done = (f32[128,128]{1,0:T(8,128)}, f32[128,128]{1,0:T(8,128)}) async-done(((f32[128,128]{1,0:T(8,128)}, f32[128,128]{1,0:T(8,128)}), (f32[128,128]{1,0:T(8,128)}, f32[128,128]{1,0:T(8,128)})) %all-reduce.12.cloned.1.call-update) | async-done | bytes 131088 | tf_op jit(solution)/shard_map/psum | solution.py:38
  323.4 1.2 fusion.11
  324.6 0.0 copy-start.3
  324.6 1.6 convolution_add_fusion.5
  326.2 0.0 copy-start.4
  326.2 1.1 fusion.14
  327.3 1.2 fusion.8
  328.5 0.0 copy-done.7
  328.5 0.5 convolution_add_fusion.2
  328.9 1.1 fusion.16
  330.1 0.0 copy-done.5
  330.1 0.0 all-reduce.10.cloned.1.call-update
  330.1 0.0 all-reduce.8.cloned.1.call-start
  330.1 70.6 %all-reduce.10.cloned.1.call-done = (f32[128,128]{1,0:T(8,128)}, f32[128,128]{1,0:T(8,128)}) async-done(((f32[128,128]{1,0:T(8,128)}, f32[128,128]{1,0:T(8,128)}), (f32[128,128]{1,0:T(8,128)}, f32[128,128]{1,0:T(8,128)})) %all-reduce.10.cloned.1.call-update) | async-done | bytes 131088 | tf_op jit(solution)/shard_map/psum | solution.py:38
  400.7 1.2 fusion.10
  401.9 0.4 convolution_add_fusion.4
  402.3 0.0 copy-done.6
  402.3 1.1 fusion.15
  403.4 1.2 fusion.7
  404.6 0.4 convolution_add_fusion.1
  405.0 1.1 fusion.17
  406.1 0.0 all-reduce.8.cloned.1.call-update
  406.1 0.0 all-gather.3.cloned.1.call-start
  406.2 70.5 %all-reduce.8.cloned.1.call-done = (f32[128,128]{1,0:T(8,128)}, f32[128,128]{1,0:T(8,128)}) async-done(((f32[128,128]{1,0:T(8,128)}, f32[128,128]{1,0:T(8,128)}), (f32[128,128]{1,0:T(8,128)}, f32[128,128]{1,0:T(8,128)})) %all-reduce.8.cloned.1.call-update) | async-done | bytes 131088 | tf_op jit(solution)/shard_map/psum | solution.py:38
  476.7 1.2 fusion.9
  477.9 0.0 copy-done.3
  477.9 1.1 fusion.5
  479.0 0.0 all-gather.3.cloned.1.call-update
  479.0 0.0 all-gather.5.cloned.1.call-start
  479.1 1.2 fusion.6
  480.2 0.0 copy-done.4
  480.3 1.1 fusion.4
  481.4 0.0 all-gather.5.cloned.1.call-update
  481.4 55.0 %all-gather.3.cloned.1.call-done = bf16[4096,640]{1,0:T(8,128)(2,1)} async-done(((bf16[128,640]{1,0:T(8,128)(2,1)}), bf16[4096,640]{1,0:T(8,128)(2,1)}) %all-gather.3.cloned.1.call-update) | async-done | bytes 5242896 | tf_op jit(solution)/shard_map/all_gather | solution.py:64
  536.4 55.3 %all-gather.5.cloned.1.call-done = bf16[4096,640]{1,0:T(8,128)(2,1)} async-done(((bf16[128,640]{1,0:T(8,128)(2,1)}), bf16[4096,640]{1,0:T(8,128)(2,1)}) %all-gather.5.cloned.1.call-update) | async-done | bytes 5242896 | tf_op jit(solution)/shard_map/all_gather | solution.py:65
  591.7 0.0 copy-start
  591.7 5.4 copy.18
  597.2 0.0 copy-done
  597.2 2.4 copy.19
Async XLA Ops:
  7.2 115.8 %reduce-scatter.3.cloned.1.call-start = ((), (), s32[]{:S(2)}) async-start(), calls=%async_computation.2 | async-start | bytes 10813440 | tf_op jit(solution)/shard_map/reduce_scatter | solution.py:57
  14.4 218.3 %reduce-scatter.5.cloned.1.call-start = ((), (), s32[]{:S(2)}) async-start(), calls=%async_computation.3 | async-start | bytes 10813440 | tf_op jit(solution)/shard_map/reduce_scatter | solution.py:58
  21.4 101.5 %copy-start.1 = (f32[128,640]{1,0:T(8,128)S(1)}, f32[128,640]{1,0:T(8,128)}, u32[]{:S(2)}) copy-start(f32[128,640]{1,0:T(8,128)} %param.8) | copy-start | bytes 983044
  21.4 211.3 %copy-start.2 = (f32[128,640]{1,0:T(8,128)S(1)}, f32[128,640]{1,0:T(8,128)}, u32[]{:S(2)}) copy-start(f32[128,640]{1,0:T(8,128)} %param.9) | copy-start | bytes 983044
  21.5 302.0 %all-reduce.12.cloned.1.call-start = ((), (), s32[]{:S(2)}) async-start(), calls=%async_computation.8 | async-start | bytes 262144 | tf_op jit(solution)/shard_map/psum | solution.py:38
  124.6 205.4 %copy-start.5 = (f32[128,640]{1,0:T(8,128)}, f32[128,640]{1,0:T(8,128)S(1)}, u32[]{:S(2)}) copy-start(f32[128,640]{1,0:T(8,128)S(1)} %get-tuple-element.20) | copy-start | bytes 983044
  232.7 95.8 %copy-start.7 = (f32[128,640]{1,0:T(8,128)S(1)}, f32[128,640]{1,0:T(8,128)}, u32[]{:S(2)}) copy-start(f32[128,640]{1,0:T(8,128)} %reduce-scatter.5.cloned.1.call-done) | copy-start | bytes 983044
  234.4 167.9 %copy-start.6 = (f32[128,640]{1,0:T(8,128)}, f32[128,640]{1,0:T(8,128)S(1)}, u32[]{:S(2)}) copy-start(f32[128,640]{1,0:T(8,128)S(1)} %get-tuple-element.21) | copy-start | bytes 983044
  254.7 146.0 %all-reduce.10.cloned.1.call-start = ((), (), s32[]{:S(2)}) async-start(), calls=%async_computation.7 | async-start | bytes 262144 | tf_op jit(solution)/shard_map/psum | solution.py:38
  324.6 153.3 %copy-start.3 = (f32[128,640]{1,0:T(8,128)S(1)}, f32[128,640]{1,0:T(8,128)}, u32[]{:S(2)}) copy-start(f32[128,640]{1,0:T(8,128)} %param.10) | copy-start | bytes 983044
  326.2 154.1 %copy-start.4 = (f32[128,640]{1,0:T(8,128)S(1)}, f32[128,640]{1,0:T(8,128)}, u32[]{:S(2)}) copy-start(f32[128,640]{1,0:T(8,128)} %param.11) | copy-start | bytes 983044
  330.1 146.6 %all-reduce.8.cloned.1.call-start = ((), (), s32[]{:S(2)}) async-start(), calls=%async_computation.6 | async-start | bytes 262144 | tf_op jit(solution)/shard_map/psum | solution.py:38
  406.1 130.2 %all-gather.3.cloned.1.call-start = ((), (), s32[]{:S(2)}) async-start(), calls=%async_computation.4 | async-start | bytes 5406720 | tf_op jit(solution)/shard_map/all_gather | solution.py:64
  479.0 112.7 %all-gather.5.cloned.1.call-start = ((), (), s32[]{:S(2)}) async-start(), calls=%async_computation.5 | async-start | bytes 5406720 | tf_op jit(solution)/shard_map/all_gather | solution.py:65
  591.7 5.4 copy-start
Sparse Core Ops, SparseCore 0:
  14.5 108.4 reduce-scatter.2
  127.6 105.0 reduce-scatter.4
  254.8 68.5 all-reduce.11
  330.2 70.4 all-reduce.9
  406.3 70.3 all-reduce.7
  480.0 56.3 all-gather.2
  539.8 51.8 all-gather.4
where the time goes:
time: 607 us; the launch traced here: 606 us
  waiting for transfers between devices  530 us (87%)
  matrix products  21 us (3%)
  other arithmetic  17.5 us (3%)
  between operations  15.6 us (3%)
  blocking collectives  14.3 us (2%)
  local copies, waits for them, and re-layouts  7.83 us (1%)
    psum x3, waiting for transfers between devices, orthogonalize(): grams = lax.psum(tuple((self_gram(x) for x in states)), 'mp')  210 us
    reduce_scatter x1, waiting for transfers between devices, body(): lax.psum_scatter(grad_out[0].astype(jnp.float32), 'dp', scatter_dimension...  108 us
    reduce_scatter x1, waiting for transfers between devices, body(): lax.psum_scatter(grad_down[0].astype(jnp.float32), 'dp', scatter_dimensio...  101 us
    all_gather x1, waiting for transfers between devices, body(): lax.all_gather(weights[1], 'dp', axis=0, tiled=True)  55.3 us
    all_gather x1, waiting for transfers between devices, body(): lax.all_gather(weights[0], 'dp', axis=0, tiled=True)  55 us
    psum x1, blocking collectives, orthogonalize(): sums = lax.psum(tuple((jnp.sum(b * b) for b in blocks)), 'mp')  14.3 us
  transfers between devices with their start and end apart: 7, of which 7 were waited for; matrix products, arithmetic and copies ran while one was open for 2% of the time, Pallas kernels for 0%

commit v1 on v0

v1 whole, which is shorter than its diff:
```python
import functools
import math

import jax
import jax.numpy as jnp
from jax import lax
from jax.experimental import pallas as pl
from jax.experimental.pallas import tpu as pltpu
from jax.sharding import PartitionSpec as P

D = 5120
BLK = 128
ITERS = 3
NX, NY, NC = 4, 4, 2
HALF = 64
QUART = 32
MESH = pl.DeviceIdType.MESH

momentum_coef = 0.95
learn_rate = 0.5
decay_rate = 0.1
coef_a = 3.4445
coef_b = -4.775
coef_c = 2.0315
norm_eps = 1e-07

WIRE = jnp.float32


def encode(x):
    return x


def decode(y):
    return y


def dot(a, b):
    return jnp.dot(a, b, precision=lax.Precision.HIGHEST, preferred_element_type=jnp.float32)


def kernel(
    nz, width,
    grad_down, grad_out, mom_down, mom_out, mas_down, mas_out,
    new_down, new_out, out_down, out_out,
    own, sib, s2, r2, s1, r1, acc, rr2, rr1, mom, mas, look, gpart, gslot, gfull,
    small_sem, own_sem, sib_ss, sib_rs,
    p1_ss, p1_rs, p2_ss, p2_rs,
    ga_ss, ga_rs, gb_ss, gb_rs,
    aa_ss, aa_rs, ab_ss, ab_rs, as_ss, as_rs,
):
    grads, moms, mass = (grad_down, grad_out), (mom_down, mom_out), (mas_down, mas_out)
    news, outs = (new_down, new_out), (out_down, out_out)
    dp, z = lax.axis_index("dp"), lax.axis_index("mp")
    c = lax.rem(dp, 2)
    chip = lax.div(dp, 2)
    y = lax.rem(chip, NY)
    x = lax.div(chip, NY)
    other = 1 - c

    def wrap(v):
        return lax.rem(v + 4, 4)

    def device(px, py, pc=c, pz=z):
        return ((px * NY + py) * NC + pc, pz)

    sibling = device(x, y, other)
    pos = ((x, y), (y, x))

    def along(h, axis, step):
        use_x = (axis == 0) == (h == 0)
        return device(wrap(x + step), y) if use_x else device(x, wrap(y + step))

    def chip_at(h, a, b):
        return (a, b) if h == 0 else (b, a)

    def remote(src, dst, ss, rs, dev):
        return pltpu.make_async_remote_copy(
            src_ref=src, dst_ref=dst, send_sem=ss, recv_sem=rs, device_id=dev, device_id_type=MESH
        )

    sends = []

    def send(src, dst, ss, rs, dev):
        copy = remote(src, dst, ss, rs, dev)
        copy.start()
        sends.append(copy)

    def landed(dst, rs):
        pltpu.make_async_copy(dst, dst, rs).wait()

    order = (2, 1, 3, 0)

    def source(m, h, da, core):
        a = wrap(pos[h][0] + da)
        if h == 0:
            return grads[m].at[a, :, core, 0:HALF, :]
        return grads[m].at[:, a, core, HALF:BLK, :]

    own_copies = {}
    for m in range(2):
        for da in order:
            for h in range(2):
                mh = 2 * m + h
                copy = pltpu.make_async_copy(source(m, h, da, c), own.at[mh, da], own_sem.at[mh, da])
                copy.start()
                own_copies[mh, da] = copy
    small = []
    for m in range(2):
        for k, (src, dst) in enumerate(((moms[m], mom.at[m]), (mass[m], mas.at[m]))):
            copy = pltpu.make_async_copy(src, dst, small_sem.at[m, k])
            copy.start()
            small.append(copy)

    barrier = pltpu.get_barrier_semaphore()
    peers = [sibling]
    for h in range(2):
        peers += [along(h, 0, 1), along(h, 0, -1)]
    peers += [device(x, y, c, lax.rem(z + k, nz)) for k in range(1, nz)]
    for peer in peers:
        pl.semaphore_signal(barrier, inc=1, device_id=peer, device_id_type=MESH)
    pl.semaphore_wait(barrier, len(peers))

    for m in range(2):
        for da in order:
            for h in range(2):
                mh = 2 * m + h
                send(source(m, h, da, other), sib.at[mh, da], sib_ss.at[mh, da], sib_rs.at[mh, da], sibling)

    def have(m, da):
        for h in range(2):
            own_copies[2 * m + h, da].wait()
            landed(sib.at[2 * m + h, da], sib_rs.at[2 * m + h, da])

    def pair(mh, da, b, lo):
        rows = pl.ds(lo, QUART)
        return own[mh, da, b, rows, :].astype(jnp.float32) + sib[mh, da, b, rows, :].astype(jnp.float32)

    def p1_far(m):
        have(m, 2)
        for h in range(2):
            mh = 2 * m + h
            for d in range(2):
                @pl.loop(0, 4)
                def _(b):
                    s2[mh, d, b] = encode(pair(mh, 2, b, QUART * d))
                send(s2.at[mh, d], r2.at[mh, d], p1_ss.at[mh, d, 0], p1_rs.at[mh, d, 0], along(h, 0, 1 - 2 * d))

    def p1_early(m):
        have(m, 1)
        have(m, 3)
        for h in range(2):
            mh = 2 * m + h
            for d in range(2):
                @pl.loop(0, 4)
                def _(b):
                    s1[mh, d, 0, b] = encode(pair(mh, 1 + 2 * d, b, QUART * (1 - d)))
                send(s1.at[mh, d, 0], r1.at[mh, d, 0], p1_ss.at[mh, d, 1], p1_rs.at[mh, d, 1], along(h, 0, 1 - 2 * d))

    def p1_late(m):
        for h in range(2):
            mh = 2 * m + h
            for d in range(2):
                landed(r2.at[mh, d], p1_rs.at[mh, d, 0])

                @pl.loop(0, 4)
                def _(b):
                    s1[mh, d, 1, b] = encode(pair(mh, 1 + 2 * d, b, QUART * d) + decode(r2[mh, d, b]))
                send(s1.at[mh, d, 1], r1.at[mh, d, 1], p1_ss.at[mh, d, 2], p1_rs.at[mh, d, 2], along(h, 0, 1 - 2 * d))

    def p1_end(m):
        have(m, 0)
        for h in range(2):
            mh = 2 * m + h
            for d in range(2):
                for e in range(2):
                    landed(r1.at[mh, d, e], p1_rs.at[mh, d, 1 + e])

            @pl.loop(0, 4)
            def _(b):
                for q in range(2):
                    acc[mh, b, pl.ds(QUART * q, QUART), :] = (
                        pair(mh, 0, b, QUART * q) + decode(r1[mh, q, 1, b]) + decode(r1[mh, 1 - q, 0, b])
                    )

    def p2_first(m):
        for h in range(2):
            mh = 2 * m + h
            at = pos[h][1]
            for d in range(2):
                to = along(h, 1, 1 - 2 * d)
                far = acc.at[mh, wrap(at + 2), pl.ds(QUART * d, QUART), :]
                send(far, rr2.at[mh, d], p2_ss.at[mh, d, 0], p2_rs.at[mh, d, 0], to)
            for d in range(2):
                to = along(h, 1, 1 - 2 * d)
                near = acc.at[mh, wrap(at + 1 - 2 * d), pl.ds(QUART * (1 - d), QUART), :]
                send(near, rr1.at[mh, d, 0], p2_ss.at[mh, d, 1], p2_rs.at[mh, d, 1], to)

    def p2_late(m):
        for h in range(2):
            mh = 2 * m + h
            for d in range(2):
                landed(rr2.at[mh, d], p2_rs.at[mh, d, 0])
                near = acc.at[mh, wrap(pos[h][1] + 1 - 2 * d), pl.ds(QUART * d, QUART), :]
                near[...] = near[...] + rr2[mh, d]
                send(near, rr1.at[mh, d, 1], p2_ss.at[mh, d, 2], p2_rs.at[mh, d, 2], along(h, 1, 1 - 2 * d))

    def p2_end(m):
        if m == 0:
            for copy in small:
                copy.wait()
        for h in range(2):
            mh = 2 * m + h
            for d in range(2):
                for e in range(2):
                    landed(rr1.at[mh, d, e], p2_rs.at[mh, d, 1 + e])
            for q in range(2):
                rows = pl.ds(HALF * h + QUART * q, QUART)
                total = acc[mh, pos[h][1], pl.ds(QUART * q, QUART), :] + rr1[mh, q, 1] + rr1[mh, 1 - q, 0]
                new = momentum_coef * mom[m, rows, :] + total
                news[m][rows, :] = new
                look[m, rows, :] = total + momentum_coef * new
        u = look[m]
        gram = lax.dot_general(
            u, u, (((1,), (1,)), ((), ())),
            precision=lax.Precision.HIGHEST, preferred_element_type=jnp.float32,
        )
        gpart[m] = gram.reshape(nz, BLK // nz, BLK)
        for k in range(1, nz):
            to = lax.rem(z + k, nz)
            send(gpart.at[m, to], gslot.at[m, k - 1], ga_ss.at[m, k - 1], ga_rs.at[m], device(x, y, c, to))

    def gram_sum(m):
        landed(gslot.at[m], ga_rs.at[m])
        total = gpart[m, z]
        for k in range(nz - 1):
            total = total + gslot[m, k]
        gfull[m, z] = total
        for k in range(1, nz):
            to = lax.rem(z + k, nz)
            send(gfull.at[m, z], gfull.at[m, z], gb_ss.at[m, k - 1], gb_rs.at[m], device(x, y, c, to))

    def update(m):
        landed(gslot.at[m], gb_rs.at[m])
        gram = gfull[m].reshape(BLK, BLK)
        eye = lax.broadcasted_iota(jnp.int32, (BLK, BLK), 0) == lax.broadcasted_iota(jnp.int32, (BLK, BLK), 1)
        diag = jnp.where(eye, gram, 0.0)
        square = jnp.sum(jnp.sum(diag, axis=1, keepdims=True), axis=0, keepdims=True)
        inv = 1.0 / (jnp.sqrt(square) + norm_eps)
        gram = gram * inv * inv
        ident = jnp.where(eye, coef_a, 0.0)
        whole = None
        for step in range(ITERS):
            factor = ident + coef_b * gram + coef_c * dot(gram, gram)
            whole = factor if whole is None else dot(factor, whole)
            if step < ITERS - 1:
                gram = dot(dot(factor, gram), factor)
        ortho = dot(whole * inv, look[m])
        scale = learn_rate * 0.2 * math.sqrt(D)
        weights = (1.0 - learn_rate * decay_rate) * mas[m] - scale * ortho
        outs[m][x, y, c] = weights.astype(jnp.bfloat16)

    def block(m, h, a, b, lo=0, n=HALF):
        px, py = chip_at(h, a, b)
        return outs[m].at[px, py, c, pl.ds(HALF * h + lo, n), :]

    def hand(m, h, k, a, b):
        ref = block(m, h, a, b)
        send(ref, ref, as_ss.at[2 * m + h, k], as_rs.at[m], sibling)

    def fan(m, h, j, a):
        mh, ref = 2 * m + h, block(m, h, a, pos[h][1])
        for d in range(2):
            send(ref, ref, ab_ss.at[mh, j, d], ab_rs.at[mh, j, d], along(h, 1, 1 - 2 * d))

    def cols(h):
        a = pos[h][0]
        return (a, wrap(a - 1), wrap(a + 1), wrap(a + 2))

    def g_start(m):
        for h in range(2):
            mh, (a, b) = 2 * m + h, pos[h]
            ref = block(m, h, a, b)
            for d in range(2):
                send(ref, ref, aa_ss.at[mh, d], aa_rs.at[mh, d], along(h, 0, 1 - 2 * d))
        for h in range(2):
            fan(m, h, 0, pos[h][0])
            hand(m, h, 0, *pos[h])

    def g_first(m):
        for h in range(2):
            mh, (a, b) = 2 * m + h, pos[h]
            for d in range(2):
                col = cols(h)[1 + d]
                ref = block(m, h, col, b)
                landed(ref, aa_rs.at[mh, d])
                part = block(m, h, col, b, QUART * d, QUART)
                send(part, part, aa_ss.at[mh, 2 + d], aa_rs.at[mh, 2 + d], along(h, 0, 1 - 2 * d))
                fan(m, h, 1 + d, col)
                hand(m, h, 1 + d, col, b)

    def g_far(m):
        for h in range(2):
            mh, (a, b) = 2 * m + h, pos[h]
            col = cols(h)[3]
            for d in range(2):
                landed(block(m, h, col, b, QUART * d, QUART), aa_rs.at[mh, 2 + d])
            fan(m, h, 3, col)
            hand(m, h, 3, col, b)

    def g_pass(m, j):
        for h in range(2):
            mh, b = 2 * m + h, pos[h][1]
            col = cols(h)[j]
            for d in range(2):
                row = wrap(b - 1 + 2 * d)
                landed(block(m, h, col, row), ab_rs.at[mh, j, d])
                part = block(m, h, col, row, QUART * d, QUART)
                send(part, part, ab_ss.at[mh, j, 2 + d], ab_rs.at[mh, j, 2 + d], along(h, 1, 1 - 2 * d))
                hand(m, h, 4 + 3 * j + d, col, row)

    def g_last(m, j):
        for h in range(2):
            mh, b = 2 * m + h, pos[h][1]
            col, row = cols(h)[j], wrap(b + 2)
            for d in range(2):
                landed(block(m, h, col, row, QUART * d, QUART), ab_rs.at[mh, j, 2 + d])
            hand(m, h, 4 + 3 * j + 2, col, row)

    p1_far(0)
    p1_early(0)
    p1_late(0)
    p1_far(1)
    p1_end(0)
    p2_first(0)
    p1_early(1)
    p2_late(0)
    p1_late(1)
    p2_end(0)
    p1_end(1)
    p2_first(1)
    gram_sum(0)
    p2_late(1)
    update(0)
    g_start(0)
    p2_end(1)
    g_first(0)
    gram_sum(1)
    g_far(0)
    g_pass(0, 0)
    update(1)
    g_start(1)
    g_last(0, 0)
    g_pass(0, 1)
    g_pass(0, 2)
    g_first(1)
    g_pass(0, 3)
    g_far(1)
    g_last(0, 1)
    g_last(0, 2)
    g_last(0, 3)
    for j in range(4):
        g_pass(1, j)
    for j in range(4):
        g_last(1, j)
    for m in range(2):
        theirs = outs[m].at[:, :, other]
        landed(theirs, as_rs.at[m])
    for copy in sends:
        copy.wait_send()


def call(nz, width, *args):
    f32, bf16 = jnp.float32, jnp.bfloat16
    dma = pltpu.SemaphoreType.DMA
    vmem = pl.BlockSpec(memory_space=pltpu.VMEM)
    hbm = pl.BlockSpec(memory_space=pl.ANY)
    out = jax.ShapeDtypeStruct((NX, NY, NC, BLK, width), bf16)
    new = jax.ShapeDtypeStruct((BLK, width), f32)
    group = BLK // nz
    return pl.pallas_call(
        functools.partial(kernel, nz, width),
        out_shape=(new, new, out, out),
        in_specs=[hbm] * 6,
        out_specs=(vmem,) * 4,
        scratch_shapes=[
            pltpu.VMEM((4, 4, 4, HALF, width), bf16),
            pltpu.VMEM((4, 4, 4, HALF, width), bf16),
            pltpu.VMEM((4, 2, 4, QUART, width), WIRE),
            pltpu.VMEM((4, 2, 4, QUART, width), WIRE),
            pltpu.VMEM((4, 2, 2, 4, QUART, width), WIRE),
            pltpu.VMEM((4, 2, 2, 4, QUART, width), WIRE),
            pltpu.VMEM((4, 4, HALF, width), f32),
            pltpu.VMEM((4, 2, QUART, width), f32),
            pltpu.VMEM((4, 2, 2, QUART, width), f32),
            pltpu.VMEM((2, BLK, width), f32),
            pltpu.VMEM((2, BLK, width), f32),
            pltpu.VMEM((2, BLK, width), f32),
            pltpu.VMEM((2, nz, group, BLK), f32),
            pltpu.VMEM((2, nz - 1, group, BLK), f32),
            pltpu.VMEM((2, nz, group, BLK), f32),
            dma((2, 2)), dma((4, 4)), dma((4, 4)), dma((4, 4)),
            dma((4, 2, 3)), dma((4, 2, 3)), dma((4, 2, 3)), dma((4, 2, 3)),
            dma((2, nz - 1)), dma((2,)), dma((2, nz - 1)), dma((2,)),
            dma((4, 4)), dma((4, 4)), dma((4, 4, 4)), dma((4, 4, 4)), dma((4, 16)), dma((2,)),
        ],
        compiler_params=pltpu.CompilerParams(
            collective_id=0, has_side_effects=True, vmem_limit_bytes=60 * 1024 * 1024
        ),
    )(*args)


def body(grad_down, grad_out, momentum_down, momentum_out, master_down, master_out):
    nz = lax.axis_size("mp")
    width = grad_down.shape[-1]
    shape = (NX, NY, NC, BLK, width)
    new_down, new_out, out_down, out_out = call(
        nz, width, grad_down.reshape(shape), grad_out.reshape(shape),
        momentum_down, momentum_out, master_down, master_out,
    )
    rows = NX * NY * NC * BLK
    return (new_down, new_out, out_down.reshape(rows, width), out_out.reshape(rows, width))


def solution(mesh):
    placed = (
        P("dp", None, "mp"),
        P("dp", None, "mp"),
        P("dp", "mp"),
        P("dp", "mp"),
        P("dp", "mp"),
        P("dp", "mp"),
    )
    return jax.shard_map(
        body,
        mesh=mesh,
        in_specs=placed,
        out_specs=(P("dp", "mp"), P("dp", "mp"), P(None, "mp"), P(None, "mp")),
        check_vma=False,
    )
```

time: 607 us -> 125 us (0.21)
  waiting for transfers between devices: 530 us -> 0 us
  Pallas kernels: 0 us -> 113 us
  matrix products: 21 us -> 0 us
  other arithmetic: 17.5 us -> 0.01 us
  between operations: 15.6 us -> 0.64 us
  blocking collectives: 14.3 us -> 0 us
    psum x3 -> x0, waiting for transfers between devices: 210 us -> none  [orthogonalize(): grams = lax.psum(tuple((self_gram(x) for x in states)), 'mp')]
    reduce_scatter x2 -> x0, waiting for transfers between devices: 210 us -> none  [the longest x1 108 us: body(): lax.psum_scatter(grad_out[0].astype(jnp.float32), 'dp', scatter_dimension...]
    pallas_call x0 -> x1, Pallas kernels: none -> 113 us  [call(): pl.pallas_call(functools.partial(kernel, nz, width), out_shape=(new, new,...]
    all_gather x2 -> x0, waiting for transfers between devices: 110 us -> none  [the longest x1 55.3 us: body(): lax.all_gather(weights[1], 'dp', axis=0, tiled=True)]
    dot_general x18 -> x0, matrix products: 21 us -> none  [the longest x6 8.99 us: self_gram(): jnp.dot(x, x.T, precision=lax.Precision.HIGHEST, preferred_element_type=j...]
    psum x1 -> x0, blocking collectives: 14.3 us -> none  [orthogonalize(): sums = lax.psum(tuple((jnp.sum(b * b) for b in blocks)), 'mp')]
    convert_element_type x2 -> x0, other arithmetic: 14.1 us -> none  [the longest x1 7.15 us: body(): grad_down[0].astype(jnp.float32)]
  transfers between devices with their start and end apart: 7 -> 0, of which waited for: 7 -> 0; matrix products, arithmetic and copies ran while one was open for 2% -> 0% of each run, Pallas kernels for 0% -> 0%
where the time goes in v1:
time: 125 us
  Pallas kernels  113 us (90%)
  local copies, waits for them, and re-layouts  11.3 us (9%)
    pallas_call x1, Pallas kernels, call(): pl.pallas_call(functools.partial(kernel, nz, width), out_shape=(new, new,...  113 us
    unnamed x8, local copies, waits for them, and re-layouts  11.3 us

profile of v1, /device:TPU:1, one launch (start us, length us, event | category | flops | bytes accessed | tf_op | source)
XLA Modules:
  0.0 124.8 jit_solution(3197607745831683278)
XLA Ops:
  0.6 112.8 %shard_map.93 = (f32[128,640]{1,0:T(8,128)}, f32[128,640]{1,0:T(8,128)}, bf16[4,4,2,128,640]{4,3,2,1,0:T(8,128)(2,1)}, bf16[4,4,2,128,640]{4,3,2,1,0:T(8,128)(2,1)}) custom-call(bf16[4,4,2,128,640]{4,3,2,1,0:T(8,128)(2,1)} %bitcast.4, bf16[4,4,2,128,640]{4,3,2,1,0:T(8,128)(2,1)} %bitcast.5, f32[128,640]{1,0:T(8,128)} %mom_down.1, f32[128,640]{1,0:T(8,128)} %mom_out.1, ...), custom_call_target="tpu_custom_call" | custom-call | tf_op jit(solution)/shard_map/pallas_call | solution.py:381
  113.5 1.7 %copy.14 = f32[128,640]{1,0:T(8,128)} copy(f32[128,640]{1,0:T(8,128)} %get-tuple-element.16) | data formatting | bytes 655360
  115.2 0.0 slice-start
  115.2 1.9 %copy.15 = f32[128,640]{1,0:T(8,128)} copy(f32[128,640]{1,0:T(8,128)} %get-tuple-element.17) | data formatting | bytes 655360
  117.1 0.0 slice-start.1
  117.1 5.4 %copy.16 = bf16[4096,640]{1,0:T(8,128)(2,1)} copy(bf16[4096,640]{1,0:T(8,128)(2,1)} %bitcast.9) | data formatting | bytes 10485760
  122.5 0.0 slice-done
  122.5 0.0 slice-done.1
  122.5 2.4 %copy.17 = bf16[4096,640]{1,0:T(8,128)(2,1)} copy(bf16[4096,640]{1,0:T(8,128)(2,1)S(1)} %bitcast.8) | data formatting | bytes 10485760
  (1 shorter events, 0.0 us)
Async XLA Ops:
  115.2 7.3 %slice-start = ((s8[5242880]{0:T(1024)(128)(4,1)}), s8[4194304]{0:T(1024)(128)(4,1)S(1)}, s32[]{:S(2)}) async-start(s8[5242880]{0:T(1024)(128)(4,1)} %bitcast.6), calls=%async_computation | async-start | bytes 8388608
  117.1 5.4 %slice-start.1 = ((s8[5242880]{0:T(1024)(128)(4,1)}), s8[1048576]{0:T(1024)(128)(4,1)S(1)}, s32[]{:S(2)}) async-start(s8[5242880]{0:T(1024)(128)(4,1)} %bitcast.6), calls=%async_computation.1 | async-start | bytes 2097152

commit v2 on v1

--- a/solution.py
+++ b/solution.py
@@ -13,6 +13,7 @@
 ITERS = 3
 NX, NY, NC = 4, 4, 2
 HALF = 64
+TOP = 6.0
 QUART = 32
 MESH = pl.DeviceIdType.MESH
 
@@ -24,15 +25,72 @@
 coef_c = 2.0315
 norm_eps = 1e-07
 
-WIRE = jnp.float32
-
-
-def encode(x):
-    return x
-
-
-def decode(y):
-    return y
+WIRE = jnp.bfloat16
+POWER = 12
+LOW, HIGH = 2.0**-10.4, 2.0**10.4
+
+
+def encode(x, bound):
+    v = jnp.abs(x) * ((HIGH - LOW) / bound) + LOW
+    v = v * v * v
+    v = v * v
+    v = v * v
+    return jnp.where(x < 0, -v, v).astype(WIRE)
+
+
+def decode(y, bound):
+    w = y.astype(jnp.float32)
+    v = jnp.exp2(jnp.log(jnp.abs(w)) * (1.0 / (POWER * math.log(2.0))))
+    v = (v - LOW) * (bound / (HIGH - LOW))
+    return jnp.where(w < 0, -v, v)
+
+
+STEPS = (
+    ("far", 0),
+    ("early", 0),
+    ("late", 0),
+    ("far", 1),
+    ("end", 0),
+    ("first2", 0),
+    ("early", 1),
+    ("late2", 0),
+    ("late", 1),
+    ("end2", 0),
+    ("gram_send", 0),
+    ("end", 1),
+    ("first2", 1),
+    ("gram_sum", 0),
+    ("late2", 1),
+    ("update", 0),
+    ("g_start", 0),
+    ("end2", 1),
+    ("gram_send", 1),
+    ("g_first", 0),
+    ("gram_sum", 1),
+    ("g_far", 0),
+    ("g_pass", 0, 0),
+    ("update", 1),
+    ("g_start", 1),
+    ("g_last", 0, 0),
+    ("g_pass", 0, 1),
+    ("g_pass", 0, 2),
+    ("g_first", 1),
+    ("g_pass", 0, 3),
+    ("g_far", 1),
+    ("g_last", 0, 1),
+    ("g_last", 0, 2),
+    ("g_last", 0, 3),
+    ("g_pass", 1, 0),
+    ("g_pass", 1, 1),
+    ("g_pass", 1, 2),
+    ("g_pass", 1, 3),
+    ("g_last", 1, 0),
+    ("g_last", 1, 1),
+    ("g_last", 1, 2),
+    ("g_last", 1, 3),
+    ("g_end", 0),
+    ("g_end", 1),
+)
 
 
 def dot(a, b):
@@ -143,7 +201,7 @@
             for d in range(2):
                 @pl.loop(0, 4)
                 def _(b):
-                    s2[mh, d, b] = encode(pair(mh, 2, b, QUART * d))
+                    s2[mh, d, b] = encode(pair(mh, 2, b, QUART * d), 2 * TOP)
                 send(s2.at[mh, d], r2.at[mh, d], p1_ss.at[mh, d, 0], p1_rs.at[mh, d, 0], along(h, 0, 1 - 2 * d))
 
     def p1_early(m):
@@ -154,7 +212,7 @@
             for d in range(2):
                 @pl.loop(0, 4)
                 def _(b):
-                    s1[mh, d, 0, b] = encode(pair(mh, 1 + 2 * d, b, QUART * (1 - d)))
+                    s1[mh, d, 0, b] = encode(pair(mh, 1 + 2 * d, b, QUART * (1 - d)), 2 * TOP)
                 send(s1.at[mh, d, 0], r1.at[mh, d, 0], p1_ss.at[mh, d, 1], p1_rs.at[mh, d, 1], along(h, 0, 1 - 2 * d))
 
     def p1_late(m):
@@ -165,7 +223,9 @@
 
                 @pl.loop(0, 4)
                 def _(b):
-                    s1[mh, d, 1, b] = encode(pair(mh, 1 + 2 * d, b, QUART * d) + decode(r2[mh, d, b]))
+                    s1[mh, d, 1, b] = encode(
+                        pair(mh, 1 + 2 * d, b, QUART * d) + decode(r2[mh, d, b], 2 * TOP), 4 * TOP
+                    )
                 send(s1.at[mh, d, 1], r1.at[mh, d, 1], p1_ss.at[mh, d, 2], p1_rs.at[mh, d, 2], along(h, 0, 1 - 2 * d))
 
     def p1_end(m):
@@ -180,7 +240,8 @@
             def _(b):
                 for q in range(2):
                     acc[mh, b, pl.ds(QUART * q, QUART), :] = (
-                        pair(mh, 0, b, QUART * q) + decode(r1[mh, q, 1, b]) + decode(r1[mh, 1 - q, 0, b])
+                        pair(mh, 0, b, QUART * q)
+                        + decode(r1[mh, q, 1, b], 4 * TOP) + decode(r1[mh, 1 - q, 0, b], 2 * TOP)
                     )
 
     def p2_first(m):
@@ -220,6 +281,8 @@
                 new = momentum_coef * mom[m, rows, :] + total
                 news[m][rows, :] = new
                 look[m, rows, :] = total + momentum_coef * new
+
+    def gram_send(m):
         u = look[m]
         gram = lax.dot_general(
             u, u, (((1,), (1,)), ((), ())),
@@ -327,45 +390,16 @@
                 landed(block(m, h, col, row, QUART * d, QUART), ab_rs.at[mh, j, 2 + d])
             hand(m, h, 4 + 3 * j + 2, col, row)
 
-    p1_far(0)
-    p1_early(0)
-    p1_late(0)
-    p1_far(1)
-    p1_end(0)
-    p2_first(0)
-    p1_early(1)
-    p2_late(0)
-    p1_late(1)
-    p2_end(0)
-    p1_end(1)
-    p2_first(1)
-    gram_sum(0)
-    p2_late(1)
-    update(0)
-    g_start(0)
-    p2_end(1)
-    g_first(0)
-    gram_sum(1)
-    g_far(0)
-    g_pass(0, 0)
-    update(1)
-    g_start(1)
-    g_last(0, 0)
-    g_pass(0, 1)
-    g_pass(0, 2)
-    g_first(1)
-    g_pass(0, 3)
-    g_far(1)
-    g_last(0, 1)
-    g_last(0, 2)
-    g_last(0, 3)
-    for j in range(4):
-        g_pass(1, j)
-    for j in range(4):
-        g_last(1, j)
-    for m in range(2):
-        theirs = outs[m].at[:, :, other]
-        landed(theirs, as_rs.at[m])
+    def g_end(m):
+        landed(outs[m].at[:, :, other], as_rs.at[m])
+
+    steps = dict(
+        far=p1_far, early=p1_early, late=p1_late, end=p1_end, first2=p2_first, late2=p2_late, end2=p2_end,
+        gram_send=gram_send, gram_sum=gram_sum, update=update, g_start=g_start, g_first=g_first, g_far=g_far,
+        g_pass=g_pass, g_last=g_last, g_end=g_end,
+    )
+    for name, *at in STEPS:
+        steps[name](*at)
     for copy in sends:
         copy.wait_send()
 
@@ -375,8 +409,8 @@
     dma = pltpu.SemaphoreType.DMA
     vmem = pl.BlockSpec(memory_space=pltpu.VMEM)
     hbm = pl.BlockSpec(memory_space=pl.ANY)
-    out = jax.ShapeDtypeStruct((NX, NY, NC, BLK, width), bf16)
-    new = jax.ShapeDtypeStruct((BLK, width), f32)
+    out = pltpu.VMEM((NX, NY, NC, BLK, width), bf16)
+    new = pltpu.VMEM((BLK, width), f32)
     group = BLK // nz
     return pl.pallas_call(
         functools.partial(kernel, nz, width),
@@ -405,19 +439,38 @@
             dma((4, 4)), dma((4, 4)), dma((4, 4, 4)), dma((4, 4, 4)), dma((4, 16)), dma((2,)),
         ],
         compiler_params=pltpu.CompilerParams(
-            collective_id=0, has_side_effects=True, vmem_limit_bytes=60 * 1024 * 1024
+            collective_id=0, has_side_effects=True, vmem_limit_bytes=44 * 1024 * 1024
         ),
     )(*args)
+
+
+def store_kernel(*refs):
+    sem = refs[-1]
+    copies = [pltpu.make_async_copy(refs[k], refs[4 + k], sem.at[k]) for k in range(4)]
+    for copy in copies:
+        copy.start()
+    for copy in copies:
+        copy.wait()
+
+
+def store(*held):
+    return pl.pallas_call(
+        store_kernel,
+        out_shape=tuple(jax.ShapeDtypeStruct(h.shape, h.dtype) for h in held),
+        in_specs=[pl.BlockSpec(memory_space=pltpu.VMEM)] * 4,
+        out_specs=(pl.BlockSpec(memory_space=pl.ANY),) * 4,
+        scratch_shapes=[pltpu.SemaphoreType.DMA((4,))],
+    )(*held)
 
 
 def body(grad_down, grad_out, momentum_down, momentum_out, master_down, master_out):
     nz = lax.axis_size("mp")
     width = grad_down.shape[-1]
     shape = (NX, NY, NC, BLK, width)
-    new_down, new_out, out_down, out_out = call(
+    new_down, new_out, out_down, out_out = store(*call(
         nz, width, grad_down.reshape(shape), grad_out.reshape(shape),
         momentum_down, momentum_out, master_down, master_out,
-    )
+    ))
     rows = NX * NY * NC * BLK
     return (new_down, new_out, out_down.reshape(rows, width), out_out.reshape(rows, width))
 

time: 125 us -> 105 us (0.84)
  Pallas kernels: 113 us -> 98.3 us
  local copies, waits for them, and re-layouts: 11.3 us -> 6.08 us
    pallas_call x1, Pallas kernels: 113 us -> 89.7 us  [call(): pl.pallas_call(functools.partial(kernel, nz, width), out_shape=(new, new,...]
    pallas_call x0 -> x1, Pallas kernels: none -> 8.57 us  [store(): pl.pallas_call(store_kernel, out_shape=tuple((jax.ShapeDtypeStruct(h.shap...]
    unnamed x8, local copies, waits for them, and re-layouts: 11.3 us -> 6.08 us
where the time goes in v2:
time: 105 us
  Pallas kernels  98.3 us (94%)
  local copies, waits for them, and re-layouts  6.08 us (6%)
    pallas_call x1, Pallas kernels, call(): pl.pallas_call(functools.partial(kernel, nz, width), out_shape=(new, new,...  89.7 us
    pallas_call x1, Pallas kernels, store(): pl.pallas_call(store_kernel, out_shape=tuple((jax.ShapeDtypeStruct(h.shap...  8.57 us
    unnamed x8, local copies, waits for them, and re-layouts  6.08 us

profile of v2, /device:TPU:1, one launch (start us, length us, event | category | flops | bytes accessed | tf_op | source)
XLA Modules:
  0.0 105.0 jit_solution(12293845446595822282)
XLA Ops:
  0.6 89.7 %shard_map.93 = (f32[128,640]{1,0:T(8,128)S(1)}, f32[128,640]{1,0:T(8,128)S(1)}, bf16[4,4,2,128,640]{4,3,2,1,0:T(8,128)(2,1)S(1)}, bf16[4,4,2,128,640]{4,3,2,1,0:T(8,128)(2,1)S(1)}) custom-call(bf16[4,4,2,128,640]{4,3,2,1,0:T(8,128)(2,1)} %bitcast.4, bf16[4,4,2,128,640]{4,3,2,1,0:T(8,128)(2,1)} %bitcast.5, f32[128,640]{1,0:T(8,128)} %mom_down.1, ...), custom_call_target="tpu_custom_call" | custom-call | tf_op jit(solution)/shard_map/pallas_call | solution.py:415
  90.4 0.0 copy-start
  90.4 2.3 %copy-done = bf16[4,4,2,128,640]{4,3,2,1,0:T(8,128)(2,1)} copy-done((bf16[4,4,2,128,640]{4,3,2,1,0:T(8,128)(2,1)}, bf16[4,4,2,128,640]{4,3,2,1,0:T(8,128)(2,1)S(1)}, u32[]{:S(2)}) %copy-start) | copy-done | bytes 5242904
  92.7 0.0 copy-start.1
  92.7 2.3 %copy-done.1 = bf16[4,4,2,128,640]{4,3,2,1,0:T(8,128)(2,1)} copy-done((bf16[4,4,2,128,640]{4,3,2,1,0:T(8,128)(2,1)}, bf16[4,4,2,128,640]{4,3,2,1,0:T(8,128)(2,1)S(1)}, u32[]{:S(2)}) %copy-start.1) | copy-done | bytes 5242904
  95.0 0.0 copy-start.2
  95.0 0.7 copy-done.2
  95.7 0.0 copy-start.3
  95.7 0.7 copy-done.3
  96.5 8.6 %shard_map.94 = (f32[128,640]{1,0:T(8,128)}, f32[128,640]{1,0:T(8,128)}, bf16[4,4,2,128,640]{4,3,2,1,0:T(8,128)(2,1)}, bf16[4,4,2,128,640]{4,3,2,1,0:T(8,128)(2,1)}) custom-call(f32[128,640]{1,0:T(8,128)} %copy-done.2, f32[128,640]{1,0:T(8,128)} %copy-done.3, bf16[4,4,2,128,640]{4,3,2,1,0:T(8,128)(2,1)} %copy-done, bf16[4,4,2,128,640]{4,3,2,1,0:T(8,128)(2,1)} %copy-done.1), custom_call_target="tpu_custom_call" | custom-call | tf_op jit(solution)/shard_map/pallas_call | solution.py:457
Async XLA Ops:
  90.4 2.3 %copy-start = (bf16[4,4,2,128,640]{4,3,2,1,0:T(8,128)(2,1)}, bf16[4,4,2,128,640]{4,3,2,1,0:T(8,128)(2,1)S(1)}, u32[]{:S(2)}) copy-start(bf16[4,4,2,128,640]{4,3,2,1,0:T(8,128)(2,1)S(1)} %get-tuple-element.14.refs_2_) | copy-start | bytes 15728644
  92.7 2.3 %copy-start.1 = (bf16[4,4,2,128,640]{4,3,2,1,0:T(8,128)(2,1)}, bf16[4,4,2,128,640]{4,3,2,1,0:T(8,128)(2,1)S(1)}, u32[]{:S(2)}) copy-start(bf16[4,4,2,128,640]{4,3,2,1,0:T(8,128)(2,1)S(1)} %get-tuple-element.15.refs_3_) | copy-start | bytes 15728644
  95.0 0.7 copy-start.2
  95.7 0.7 copy-start.3

commit v3 on v2

--- a/solution.py
+++ b/solution.py
@@ -460,6 +460,7 @@
         in_specs=[pl.BlockSpec(memory_space=pltpu.VMEM)] * 4,
         out_specs=(pl.BlockSpec(memory_space=pl.ANY),) * 4,
         scratch_shapes=[pltpu.SemaphoreType.DMA((4,))],
+        compiler_params=pltpu.CompilerParams(vmem_limit_bytes=1024 * 1024),
     )(*held)
 
 

time: 105 us -> 94.8 us (0.903)
  local copies, waits for them, and re-layouts: 6.08 us -> 0 us
  Pallas kernels: 98.3 us -> 94.1 us
    unnamed x8 -> x0, local copies, waits for them, and re-layouts: 6.08 us -> none
    pallas_call x1, Pallas kernels: 8.57 us -> 4.34 us  [store(): pl.pallas_call(store_kernel, out_shape=tuple((jax.ShapeDtypeStruct(h.shap...]
where the time goes in v3:
time: 94.8 us; the launch traced here: 94.7 us
  Pallas kernels  94.1 us (99%)
    pallas_call x1, Pallas kernels, call(): pl.pallas_call(functools.partial(kernel, nz, width), out_shape=(new, new,...  89.7 us
    pallas_call x1, Pallas kernels, store(): pl.pallas_call(store_kernel, out_shape=tuple((jax.ShapeDtypeStruct(h.shap...  4.34 us

profile of v3, /device:TPU:1, one launch (start us, length us, event | category | flops | bytes accessed | tf_op | source)
XLA Modules:
  0.0 94.7 jit_solution(10266148677741522970)
XLA Ops:
  0.6 89.7 %shard_map.93 = (f32[128,640]{1,0:T(8,128)S(1)}, f32[128,640]{1,0:T(8,128)S(1)}, bf16[4,4,2,128,640]{4,3,2,1,0:T(8,128)(2,1)S(1)}, bf16[4,4,2,128,640]{4,3,2,1,0:T(8,128)(2,1)S(1)}) custom-call(bf16[4,4,2,128,640]{4,3,2,1,0:T(8,128)(2,1)} %bitcast.4, bf16[4,4,2,128,640]{4,3,2,1,0:T(8,128)(2,1)} %bitcast.5, f32[128,640]{1,0:T(8,128)} %mom_down.1, ...), custom_call_target="tpu_custom_call" | custom-call | tf_op jit(solution)/shard_map/pallas_call | solution.py:415
  90.4 4.3 %shard_map.94 = (f32[128,640]{1,0:T(8,128)}, f32[128,640]{1,0:T(8,128)}, bf16[4,4,2,128,640]{4,3,2,1,0:T(8,128)(2,1)}, bf16[4,4,2,128,640]{4,3,2,1,0:T(8,128)(2,1)}) custom-call(f32[128,640]{1,0:T(8,128)S(1)} %get-tuple-element.12.refs_0_, f32[128,640]{1,0:T(8,128)S(1)} %get-tuple-element.13.refs_1_, ...), custom_call_target="tpu_custom_call" | custom-call | tf_op jit(solution)/shard_map/pallas_call | solution.py:457

commit v4 on v3

v4 whole, which is shorter than its diff:
```python
import functools
import math

import jax
import jax.numpy as jnp
from jax import lax
from jax.experimental import pallas as pl
from jax.experimental.pallas import tpu as pltpu
from jax.sharding import PartitionSpec as P

D = 5120
BLK = 128
ITERS = 3
NX, NY, NC = 4, 4, 2
HALF = 64
TOP = 6.0
QUART = 32
MESH = pl.DeviceIdType.MESH

momentum_coef = 0.95
learn_rate = 0.5
decay_rate = 0.1
coef_a = 3.4445
coef_b = -4.775
coef_c = 2.0315
norm_eps = 1e-07

WIRE = jnp.bfloat16
POWER = 12
LOW, HIGH = 2.0**-10.4, 2.0**10.4


def encode(x, bound):
    v = jnp.abs(x) * ((HIGH - LOW) / bound) + LOW
    v = v * v * v
    v = v * v
    v = v * v
    return jnp.where(x < 0, -v, v).astype(WIRE)


def decode(y, bound):
    w = y.astype(jnp.float32)
    v = jnp.exp2(jnp.log(jnp.abs(w)) * (1.0 / (POWER * math.log(2.0))))
    v = (v - LOW) * (bound / (HIGH - LOW))
    return jnp.where(w < 0, -v, v)


STEPS = (
    ("far", 0, 0),
    ("far", 0, 1),
    ("early", 0, 1),
    ("early", 0, 0),
    ("late", 0, 0),
    ("late", 0, 1),
    ("far", 1, 0),
    ("end_early", 0, 1),
    ("far", 1, 1),
    ("end_early", 0, 0),
    ("end_late", 0, 0),
    ("far2", 0, 0),
    ("early2", 0, 0),
    ("end_late", 0, 1),
    ("far2", 0, 1),
    ("early2", 0, 1),
    ("early", 1, 1),
    ("early", 1, 0),
    ("late2", 0, 1),
    ("late2", 0, 0),
    ("late", 1, 1),
    ("late", 1, 0),
    ("end_early", 1, 0),
    ("end2", 0, 0),
    ("end2", 0, 1),
    ("gram_send", 0),
    ("end_early", 1, 1),
    ("end_late", 1, 1),
    ("far2", 1, 1),
    ("end_late", 1, 0),
    ("far2", 1, 0),
    ("early2", 1, 0),
    ("gram_sum", 0),
    ("early2", 1, 1),
    ("late2", 1, 1),
    ("late2", 1, 0),
    ("end2", 1, 1),
    ("upd0", 0),
    ("end2", 1, 0),
    ("gram_send", 1),
    ("upd1", 0),
    ("upd2", 0),
    ("g_own", 0, 1),
    ("g_own", 0, 0),
    ("g_fan", 0, 1, 0),
    ("g_fan", 0, 0, 0),
    ("gram_sum", 1),
    ("g_near", 0, 1),
    ("g_near", 0, 0),
    ("g_fan", 0, 0, 1),
    ("g_fan", 0, 1, 1),
    ("g_pass", 0, 0, 0),
    ("g_fan", 0, 0, 2),
    ("g_fan", 0, 1, 2),
    ("g_fan", 0, 0, 3),
    ("g_pass", 0, 1, 0),
    ("g_fan", 0, 1, 3),
    ("upd0", 1),
    ("upd1", 1),
    ("upd2", 1),
    ("g_own", 1, 0),
    ("g_own", 1, 1),
    ("g_fan", 1, 0, 0),
    ("g_pass", 0, 1, 1),
    ("g_last", 0, 1, 0),
    ("g_pass", 0, 0, 2),
    ("g_fan", 1, 1, 0),
    ("g_near", 1, 1),
    ("g_near", 1, 0),
    ("g_fan", 1, 0, 2),
    ("g_fan", 1, 1, 1),
    ("g_fan", 1, 0, 1),
    ("g_fan", 1, 1, 2),
    ("g_pass", 0, 1, 2),
    ("g_fan", 1, 0, 3),
    ("g_pass", 0, 0, 3),
    ("g_fan", 1, 1, 3),
    ("g_pass", 0, 1, 3),
    ("g_pass", 0, 0, 1),
    ("g_pass", 1, 0, 1),
    ("g_pass", 1, 1, 0),
    ("g_pass", 1, 1, 2),
    ("g_pass", 1, 0, 0),
    ("g_pass", 1, 0, 3),
    ("g_last", 0, 1, 1),
    ("g_pass", 1, 0, 2),
    ("g_last", 0, 0, 0),
    ("g_pass", 1, 1, 1),
    ("g_pass", 1, 1, 3),
    ("g_last", 0, 0, 2),
    ("g_last", 1, 0, 1),
    ("g_last", 1, 1, 2),
    ("g_last", 0, 1, 3),
    ("g_last", 0, 1, 2),
    ("g_last", 1, 0, 0),
    ("g_last", 1, 1, 0),
    ("g_last", 0, 0, 3),
    ("g_last", 0, 0, 1),
    ("g_last", 1, 1, 1),
    ("g_last", 1, 0, 3),
    ("g_last", 1, 0, 2),
    ("g_last", 1, 1, 3),
    ("g_end", 1),
    ("g_end", 0),
)


def dot(a, b):
    return jnp.dot(a, b, precision=lax.Precision.HIGHEST, preferred_element_type=jnp.float32)


def kernel(
    nz, width,
    grad_down, grad_out, mom_down, mom_out, mas_down, mas_out,
    new_down, new_out, out_down, out_out,
    own, sib, s2, r2, s1, r1, acc, t2, rr2, t1, rr1, whole, power, mom, mas, look, gpart, gslot, gfull,
    small_sem, own_sem, sib_ss, sib_rs,
    p1_ss, p1_rs, p2_ss, p2_rs,
    ga_ss, ga_rs, gb_ss, gb_rs,
    aa_ss, aa_rs, ab_ss, ab_rs, as_ss, as_rs,
):
    grads, moms, mass = (grad_down, grad_out), (mom_down, mom_out), (mas_down, mas_out)
    news, outs = (new_down, new_out), (out_down, out_out)
    dp, z = lax.axis_index("dp"), lax.axis_index("mp")
    c = lax.rem(dp, 2)
    chip = lax.div(dp, 2)
    y = lax.rem(chip, NY)
    x = lax.div(chip, NY)
    other = 1 - c

    def wrap(v):
        return lax.rem(v + 4, 4)

    def device(px, py, pc=c, pz=z):
        return ((px * NY + py) * NC + pc, pz)

    sibling = device(x, y, other)
    pos = ((x, y), (y, x))

    def along(h, axis, step):
        use_x = (axis == 0) == (h == 0)
        return device(wrap(x + step), y) if use_x else device(x, wrap(y + step))

    def chip_at(h, a, b):
        return (a, b) if h == 0 else (b, a)

    def remote(src, dst, ss, rs, dev):
        return pltpu.make_async_remote_copy(
            src_ref=src, dst_ref=dst, send_sem=ss, recv_sem=rs, device_id=dev, device_id_type=MESH
        )

    sends = []

    def send(src, dst, ss, rs, dev):
        copy = remote(src, dst, ss, rs, dev)
        copy.start()
        sends.append(copy)

    def landed(dst, rs):
        pltpu.make_async_copy(dst, dst, rs).wait()

    order = (2, 1, 3, 0)

    def source(m, h, da, core):
        a = wrap(pos[h][0] + da)
        if h == 0:
            return grads[m].at[a, :, core, 0:HALF, :]
        return grads[m].at[:, a, core, HALF:BLK, :]

    own_copies = {}
    for m in range(2):
        for da in order:
            for h in range(2):
                mh = 2 * m + h
                copy = pltpu.make_async_copy(source(m, h, da, c), own.at[mh, da], own_sem.at[mh, da])
                copy.start()
                own_copies[mh, da] = copy
    small = []
    for m in range(2):
        for k, (src, dst) in enumerate(((moms[m], mom.at[m]), (mass[m], mas.at[m]))):
            copy = pltpu.make_async_copy(src, dst, small_sem.at[m, k])
            copy.start()
            small.append(copy)

    barrier = pltpu.get_barrier_semaphore()
    peers = [sibling]
    for h in range(2):
        peers += [along(h, 0, 1), along(h, 0, -1)]
    peers += [device(x, y, c, lax.rem(z + k, nz)) for k in range(1, nz)]
    for peer in peers:
        pl.semaphore_signal(barrier, inc=1, device_id=peer, device_id_type=MESH)
    pl.semaphore_wait(barrier, len(peers))

    for m in range(2):
        for da in order:
            for h in range(2):
                mh = 2 * m + h
                send(source(m, h, da, other), sib.at[mh, da], sib_ss.at[mh, da], sib_rs.at[mh, da], sibling)

    def have(m, h, da):
        own_copies[2 * m + h, da].wait()
        landed(sib.at[2 * m + h, da], sib_rs.at[2 * m + h, da])

    def pair(mh, da, b, lo):
        rows = pl.ds(lo, QUART)
        return own[mh, da, b, rows, :].astype(jnp.float32) + sib[mh, da, b, rows, :].astype(jnp.float32)

    def far(m, h):
        have(m, h, 2)
        mh = 2 * m + h
        for d in range(2):
            @pl.loop(0, 4)
            def _(b):
                s2[mh, d, b] = encode(pair(mh, 2, b, QUART * d), 2 * TOP)
            send(s2.at[mh, d], r2.at[mh, d], p1_ss.at[mh, d, 0], p1_rs.at[mh, d, 0], along(h, 0, 1 - 2 * d))

    def early(m, h):
        mh = 2 * m + h
        for d in range(2):
            have(m, h, 1 + 2 * d)

            @pl.loop(0, 4)
            def _(b):
                s1[mh, d, 0, b] = encode(pair(mh, 1 + 2 * d, b, QUART * (1 - d)), 2 * TOP)
            send(s1.at[mh, d, 0], r1.at[mh, d, 0], p1_ss.at[mh, d, 1], p1_rs.at[mh, d, 1], along(h, 0, 1 - 2 * d))

    def late(m, h):
        mh = 2 * m + h
        for d in range(2):
            landed(r2.at[mh, d], p1_rs.at[mh, d, 0])

            @pl.loop(0, 4)
            def _(b):
                s1[mh, d, 1, b] = encode(
                    pair(mh, 1 + 2 * d, b, QUART * d) + decode(r2[mh, d, b], 2 * TOP), 4 * TOP
                )
            send(s1.at[mh, d, 1], r1.at[mh, d, 1], p1_ss.at[mh, d, 2], p1_rs.at[mh, d, 2], along(h, 0, 1 - 2 * d))

    def end_early(m, h):
        have(m, h, 0)
        mh = 2 * m + h
        for d in range(2):
            landed(r1.at[mh, d, 0], p1_rs.at[mh, d, 1])

        @pl.loop(0, 4)
        def _(b):
            for q in range(2):
                acc[mh, b, pl.ds(QUART * q, QUART), :] = (
                    pair(mh, 0, b, QUART * q) + decode(r1[mh, 1 - q, 0, b], 2 * TOP)
                )

    def end_late(m, h):
        mh = 2 * m + h
        for d in range(2):
            landed(r1.at[mh, d, 1], p1_rs.at[mh, d, 2])

        @pl.loop(0, 4)
        def _(b):
            for q in range(2):
                rows = pl.ds(QUART * q, QUART)
                acc[mh, b, rows, :] = acc[mh, b, rows, :] + decode(r1[mh, q, 1, b], 4 * TOP)

    def far2(m, h):
        mh, at = 2 * m + h, pos[h][1]
        for d in range(2):
            t2[mh, d] = encode(acc[mh, wrap(at + 2), pl.ds(QUART * d, QUART), :], 8 * TOP)
            send(t2.at[mh, d], rr2.at[mh, d], p2_ss.at[mh, d, 0], p2_rs.at[mh, d, 0], along(h, 1, 1 - 2 * d))

    def early2(m, h):
        mh, at = 2 * m + h, pos[h][1]
        for d in range(2):
            near = acc[mh, wrap(at + 1 - 2 * d), pl.ds(QUART * (1 - d), QUART), :]
            t1[mh, d, 0] = encode(near, 8 * TOP)
            send(t1.at[mh, d, 0], rr1.at[mh, d, 0], p2_ss.at[mh, d, 1], p2_rs.at[mh, d, 1], along(h, 1, 1 - 2 * d))

    def late2(m, h):
        mh = 2 * m + h
        for d in range(2):
            landed(rr2.at[mh, d], p2_rs.at[mh, d, 0])
            near = acc[mh, wrap(pos[h][1] + 1 - 2 * d), pl.ds(QUART * d, QUART), :]
            t1[mh, d, 1] = encode(near + decode(rr2[mh, d], 8 * TOP), 16 * TOP)
            send(t1.at[mh, d, 1], rr1.at[mh, d, 1], p2_ss.at[mh, d, 2], p2_rs.at[mh, d, 2], along(h, 1, 1 - 2 * d))

    def end2(m, h):
        if m == 0 and h == 0:
            for copy in small:
                copy.wait()
        mh = 2 * m + h
        for d in range(2):
            for e in range(2):
                landed(rr1.at[mh, d, e], p2_rs.at[mh, d, 1 + e])
        for q in range(2):
            rows = pl.ds(HALF * h + QUART * q, QUART)
            total = (
                acc[mh, pos[h][1], pl.ds(QUART * q, QUART), :]
                + decode(rr1[mh, q, 1], 16 * TOP) + decode(rr1[mh, 1 - q, 0], 8 * TOP)
            )
            new = momentum_coef * mom[m, rows, :] + total
            news[m][rows, :] = new
            look[m, rows, :] = total + momentum_coef * new

    def gram_send(m):
        u = look[m]
        gram = lax.dot_general(
            u, u, (((1,), (1,)), ((), ())),
            precision=lax.Precision.HIGHEST, preferred_element_type=jnp.float32,
        )
        gpart[m] = gram.reshape(nz, BLK // nz, BLK)
        for k in range(1, nz):
            to = lax.rem(z + k, nz)
            send(gpart.at[m, to], gslot.at[m, k - 1], ga_ss.at[m, k - 1], ga_rs.at[m], device(x, y, c, to))

    def gram_sum(m):
        landed(gslot.at[m], ga_rs.at[m])
        total = gpart[m, z]
        for k in range(nz - 1):
            total = total + gslot[m, k]
        gfull[m, z] = total
        for k in range(1, nz):
            to = lax.rem(z + k, nz)
            send(gfull.at[m, z], gfull.at[m, z], gb_ss.at[m, k - 1], gb_rs.at[m], device(x, y, c, to))

    def upd0(m):
        landed(gslot.at[m], gb_rs.at[m])
        gram = gfull[m].reshape(BLK, BLK)
        eye = lax.broadcasted_iota(jnp.int32, (BLK, BLK), 0) == lax.broadcasted_iota(jnp.int32, (BLK, BLK), 1)
        diag = jnp.where(eye, gram, 0.0)
        square = jnp.sum(jnp.sum(diag, axis=1, keepdims=True), axis=0, keepdims=True)
        inv = 1.0 / (jnp.sqrt(square) + norm_eps)
        gram = gram * inv * inv
        factor = jnp.where(eye, coef_a, 0.0) + coef_b * gram + coef_c * dot(gram, gram)
        whole[m] = factor * inv
        power[m] = dot(dot(factor, gram), factor)

    def factor_of(gram):
        eye = lax.broadcasted_iota(jnp.int32, (BLK, BLK), 0) == lax.broadcasted_iota(jnp.int32, (BLK, BLK), 1)
        return jnp.where(eye, coef_a, 0.0) + coef_b * gram + coef_c * dot(gram, gram)

    def upd1(m):
        gram = power[m]
        factor = factor_of(gram)
        whole[m] = dot(factor, whole[m])
        power[m] = dot(dot(factor, gram), factor)

    def upd2(m):
        ortho = dot(dot(factor_of(power[m]), whole[m]), look[m])
        scale = learn_rate * 0.2 * math.sqrt(D)
        weights = (1.0 - learn_rate * decay_rate) * mas[m] - scale * ortho
        outs[m][x, y, c] = weights.astype(jnp.bfloat16)

    def block(m, h, a, b, lo=0, n=HALF):
        px, py = chip_at(h, a, b)
        return outs[m].at[px, py, c, pl.ds(HALF * h + lo, n), :]

    def hand(m, h, k, a, b):
        ref = block(m, h, a, b)
        send(ref, ref, as_ss.at[2 * m + h, k], as_rs.at[m], sibling)

    def fan(m, h, j, a):
        mh, ref = 2 * m + h, block(m, h, a, pos[h][1])
        for d in range(2):
            send(ref, ref, ab_ss.at[mh, j, d], ab_rs.at[mh, j, d], along(h, 1, 1 - 2 * d))

    def cols(h):
        a = pos[h][0]
        return (a, wrap(a - 1), wrap(a + 1), wrap(a + 2))

    def g_own(m, h):
        ref = block(m, h, *pos[h])
        for d in range(2):
            send(ref, ref, aa_ss.at[2 * m + h, d], aa_rs.at[2 * m + h, d], along(h, 0, 1 - 2 * d))

    def g_near(m, h):
        mh, b = 2 * m + h, pos[h][1]
        for d in range(2):
            col = cols(h)[1 + d]
            landed(block(m, h, col, b), aa_rs.at[mh, d])
            part = block(m, h, col, b, QUART * d, QUART)
            send(part, part, aa_ss.at[mh, 2 + d], aa_rs.at[mh, 2 + d], along(h, 0, 1 - 2 * d))

    def g_fan(m, h, j):
        mh, b = 2 * m + h, pos[h][1]
        col = cols(h)[j]
        if j == 3:
            for d in range(2):
                landed(block(m, h, col, b, QUART * d, QUART), aa_rs.at[mh, 2 + d])
        fan(m, h, j, col)
        hand(m, h, j, col, b)

    def g_pass(m, h, j):
        mh, b = 2 * m + h, pos[h][1]
        col = cols(h)[j]
        for d in range(2):
            row = wrap(b - 1 + 2 * d)
            landed(block(m, h, col, row), ab_rs.at[mh, j, d])
            part = block(m, h, col, row, QUART * d, QUART)
            send(part, part, ab_ss.at[mh, j, 2 + d], ab_rs.at[mh, j, 2 + d], along(h, 1, 1 - 2 * d))
            hand(m, h, 4 + 3 * j + d, col, row)

    def g_last(m, h, j):
        mh, b = 2 * m + h, pos[h][1]
        col, row = cols(h)[j], wrap(b + 2)
        for d in range(2):
            landed(block(m, h, col, row, QUART * d, QUART), ab_rs.at[mh, j, 2 + d])
        hand(m, h, 4 + 3 * j + 2, col, row)

    def g_end(m):
        landed(outs[m].at[:, :, other], as_rs.at[m])

    steps = dict(
        far=far, early=early, late=late, end_early=end_early, end_late=end_late,
        far2=far2, early2=early2, late2=late2, end2=end2,
        gram_send=gram_send, gram_sum=gram_sum, upd0=upd0, upd1=upd1, upd2=upd2,
        g_own=g_own, g_near=g_near, g_fan=g_fan, g_pass=g_pass, g_last=g_last, g_end=g_end,
    )
    for name, *at in STEPS:
        steps[name](*at)
    for copy in sends:
        copy.wait_send()


def call(nz, width, *args):
    f32, bf16 = jnp.float32, jnp.bfloat16
    dma = pltpu.SemaphoreType.DMA
    vmem = pl.BlockSpec(memory_space=pltpu.VMEM)
    hbm = pl.BlockSpec(memory_space=pl.ANY)
    out = pltpu.VMEM((NX, NY, NC, BLK, width), bf16)
    new = pltpu.VMEM((BLK, width), f32)
    group = BLK // nz
    return pl.pallas_call(
        functools.partial(kernel, nz, width),
        out_shape=(new, new, out, out),
        in_specs=[hbm] * 6,
        out_specs=(vmem,) * 4,
        scratch_shapes=[
            pltpu.VMEM((4, 4, 4, HALF, width), bf16),
            pltpu.VMEM((4, 4, 4, HALF, width), bf16),
            pltpu.VMEM((4, 2, 4, QUART, width), WIRE),
            pltpu.VMEM((4, 2, 4, QUART, width), WIRE),
            pltpu.VMEM((4, 2, 2, 4, QUART, width), WIRE),
            pltpu.VMEM((4, 2, 2, 4, QUART, width), WIRE),
            pltpu.VMEM((4, 4, HALF, width), f32),
            pltpu.VMEM((4, 2, QUART, width), WIRE),
            pltpu.VMEM((4, 2, QUART, width), WIRE),
            pltpu.VMEM((4, 2, 2, QUART, width), WIRE),
            pltpu.VMEM((4, 2, 2, QUART, width), WIRE),
            pltpu.VMEM((2, BLK, BLK), f32),
            pltpu.VMEM((2, BLK, BLK), f32),
            pltpu.VMEM((2, BLK, width), f32),
            pltpu.VMEM((2, BLK, width), f32),
            pltpu.VMEM((2, BLK, width), f32),
            pltpu.VMEM((2, nz, group, BLK), f32),
            pltpu.VMEM((2, nz - 1, group, BLK), f32),
            pltpu.VMEM((2, nz, group, BLK), f32),
            dma((2, 2)), dma((4, 4)), dma((4, 4)), dma((4, 4)),
            dma((4, 2, 3)), dma((4, 2, 3)), dma((4, 2, 3)), dma((4, 2, 3)),
            dma((2, nz - 1)), dma((2,)), dma((2, nz - 1)), dma((2,)),
            dma((4, 4)), dma((4, 4)), dma((4, 4, 4)), dma((4, 4, 4)), dma((4, 16)), dma((2,)),
        ],
        compiler_params=pltpu.CompilerParams(
            collective_id=0, has_side_effects=True, vmem_limit_bytes=44 * 1024 * 1024
        ),
    )(*args)


def store_kernel(*refs):
    sem = refs[-1]
    copies = [pltpu.make_async_copy(refs[k], refs[4 + k], sem.at[k]) for k in range(2)]
    for k in range(2, 4):
        for i in range(NX):
            copies.append(pltpu.make_async_copy(refs[k].at[i], refs[4 + k].at[i], sem.at[NX * (k - 1) + i]))
    for copy in copies:
        copy.start()
    for copy in copies:
        copy.wait()


def store(*held):
    return pl.pallas_call(
        store_kernel,
        out_shape=tuple(jax.ShapeDtypeStruct(h.shape, h.dtype) for h in held),
        in_specs=[pl.BlockSpec(memory_space=pltpu.VMEM)] * 4,
        out_specs=(pl.BlockSpec(memory_space=pl.ANY),) * 4,
        scratch_shapes=[pltpu.SemaphoreType.DMA((3 * NX,))],
        compiler_params=pltpu.CompilerParams(vmem_limit_bytes=1024 * 1024),
    )(*held)


def body(grad_down, grad_out, momentum_down, momentum_out, master_down, master_out):
    nz = lax.axis_size("mp")
    width = grad_down.shape[-1]
    shape = (NX, NY, NC, BLK, width)
    new_down, new_out, out_down, out_out = store(*call(
        nz, width, grad_down.reshape(shape), grad_out.reshape(shape),
        momentum_down, momentum_out, master_down, master_out,
    ))
    rows = NX * NY * NC * BLK
    return (new_down, new_out, out_down.reshape(rows, width), out_out.reshape(rows, width))


def solution(mesh):
    placed = (
        P("dp", None, "mp"),
        P("dp", None, "mp"),
        P("dp", "mp"),
        P("dp", "mp"),
        P("dp", "mp"),
        P("dp", "mp"),
    )
    return jax.shard_map(
        body,
        mesh=mesh,
        in_specs=placed,
        out_specs=(P("dp", "mp"), P("dp", "mp"), P(None, "mp"), P(None, "mp")),
        check_vma=False,
    )
```

time: 94.8 us -> 90.1 us (0.950)
  Pallas kernels: 94.1 us -> 89.3 us
    pallas_call x1, Pallas kernels: 89.7 us -> 85.1 us  [call(): pl.pallas_call(functools.partial(kernel, nz, width), out_shape=(new, new,...]
where the time goes in v4:
time: 90.1 us; the launch traced here: 90 us
  Pallas kernels  89.3 us (99%)
    pallas_call x1, Pallas kernels, call(): pl.pallas_call(functools.partial(kernel, nz, width), out_shape=(new, new,...  85.1 us
    pallas_call x1, Pallas kernels, store(): pl.pallas_call(store_kernel, out_shape=tuple((jax.ShapeDtypeStruct(h.shap...  4.25 us

profile of v4, /device:TPU:1, one launch (start us, length us, event | category | flops | bytes accessed | tf_op | source)
XLA Modules:
  0.0 90.0 jit_solution(16283904504140038166)
XLA Ops:
  0.6 85.1 %shard_map.93 = (f32[128,640]{1,0:T(8,128)S(1)}, f32[128,640]{1,0:T(8,128)S(1)}, bf16[4,4,2,128,640]{4,3,2,1,0:T(8,128)(2,1)S(1)}, bf16[4,4,2,128,640]{4,3,2,1,0:T(8,128)(2,1)S(1)}) custom-call(bf16[4,4,2,128,640]{4,3,2,1,0:T(8,128)(2,1)} %bitcast.4, bf16[4,4,2,128,640]{4,3,2,1,0:T(8,128)(2,1)} %bitcast.5, f32[128,640]{1,0:T(8,128)} %mom_down.1, ...), custom_call_target="tpu_custom_call" | custom-call | tf_op jit(solution)/shard_map/pallas_call | solution.py:478
  85.7 4.2 %shard_map.94 = (f32[128,640]{1,0:T(8,128)}, f32[128,640]{1,0:T(8,128)}, bf16[4,4,2,128,640]{4,3,2,1,0:T(8,128)(2,1)}, bf16[4,4,2,128,640]{4,3,2,1,0:T(8,128)(2,1)}) custom-call(f32[128,640]{1,0:T(8,128)S(1)} %get-tuple-element.12.refs_0_, f32[128,640]{1,0:T(8,128)S(1)} %get-tuple-element.13.refs_1_, ...), custom_call_target="tpu_custom_call" | custom-call | tf_op jit(solution)/shard_map/pallas_call | solution.py:527

commit v5 on v4

--- a/solution.py
+++ b/solution.py
@@ -15,6 +15,7 @@
 HALF = 64
 TOP = 6.0
 QUART = 32
+SPLIT = 2
 MESH = pl.DeviceIdType.MESH
 
 momentum_coef = 0.95
@@ -46,110 +47,130 @@
 
 
 STEPS = (
-    ("far", 0, 0),
-    ("far", 0, 1),
-    ("early", 0, 1),
-    ("early", 0, 0),
-    ("late", 0, 0),
-    ("late", 0, 1),
-    ("far", 1, 0),
-    ("end_early", 0, 1),
-    ("far", 1, 1),
-    ("end_early", 0, 0),
-    ("end_late", 0, 0),
+    ("far", 0, 0, 0),
+    ("far", 0, 1, 0),
+    ("far", 0, 0, 1),
+    ("far", 0, 1, 1),
+    ("early", 0, 0, 0),
+    ("early", 0, 1, 0),
+    ("late", 0, 0, 0),
+    ("late", 0, 1, 0),
+    ("early", 0, 0, 1),
+    ("late", 0, 0, 1),
+    ("early", 0, 1, 1),
+    ("late", 0, 1, 1),
+    ("end_early", 0, 0, 0),
+    ("end_late", 0, 0, 0),
     ("far2", 0, 0),
+    ("end_early", 0, 1, 0),
+    ("end_late", 0, 1, 0),
+    ("far2", 0, 1),
+    ("far", 1, 1, 0),
+    ("far", 1, 0, 0),
+    ("end_early", 0, 0, 1),
+    ("end_early", 0, 1, 1),
+    ("end_late", 0, 0, 1),
     ("early2", 0, 0),
-    ("end_late", 0, 1),
-    ("far2", 0, 1),
+    ("end_late", 0, 1, 1),
     ("early2", 0, 1),
-    ("early", 1, 1),
-    ("early", 1, 0),
+    ("late2", 0, 0),
     ("late2", 0, 1),
-    ("late2", 0, 0),
-    ("late", 1, 1),
-    ("late", 1, 0),
-    ("end_early", 1, 0),
+    ("early", 1, 1, 0),
+    ("far", 1, 0, 1),
+    ("early", 1, 0, 0),
+    ("late", 1, 0, 0),
+    ("far", 1, 1, 1),
+    ("late", 1, 1, 0),
     ("end2", 0, 0),
     ("end2", 0, 1),
     ("gram_send", 0),
-    ("end_early", 1, 1),
-    ("end_late", 1, 1),
+    ("early", 1, 1, 1),
+    ("early", 1, 0, 1),
+    ("late", 1, 1, 1),
+    ("end_early", 1, 0, 0),
+    ("late", 1, 0, 1),
+    ("end_early", 1, 1, 0),
+    ("end_late", 1, 0, 0),
+    ("far2", 1, 0),
+    ("gram_sum", 0),
+    ("end_late", 1, 1, 0),
     ("far2", 1, 1),
-    ("end_late", 1, 0),
-    ("far2", 1, 0),
+    ("end_early", 1, 1, 1),
+    ("end_late", 1, 1, 1),
+    ("end_early", 1, 0, 1),
+    ("end_late", 1, 0, 1),
+    ("early2", 1, 1),
     ("early2", 1, 0),
-    ("gram_sum", 0),
-    ("early2", 1, 1),
+    ("late2", 1, 0),
     ("late2", 1, 1),
-    ("late2", 1, 0),
-    ("end2", 1, 1),
     ("upd0", 0),
-    ("end2", 1, 0),
-    ("gram_send", 1),
     ("upd1", 0),
     ("upd2", 0),
     ("g_own", 0, 1),
     ("g_own", 0, 0),
+    ("end2", 1, 0),
+    ("end2", 1, 1),
+    ("gram_send", 1),
     ("g_fan", 0, 1, 0),
     ("g_fan", 0, 0, 0),
-    ("gram_sum", 1),
     ("g_near", 0, 1),
     ("g_near", 0, 0),
-    ("g_fan", 0, 0, 1),
-    ("g_fan", 0, 1, 1),
-    ("g_pass", 0, 0, 0),
     ("g_fan", 0, 0, 2),
     ("g_fan", 0, 1, 2),
+    ("g_fan", 0, 1, 1),
+    ("g_fan", 0, 0, 1),
+    ("gram_sum", 1),
+    ("g_pass", 0, 1, 2),
+    ("g_pass", 0, 0, 2),
+    ("g_pass", 0, 0, 0),
+    ("g_fan", 0, 1, 3),
+    ("g_pass", 0, 1, 0),
     ("g_fan", 0, 0, 3),
-    ("g_pass", 0, 1, 0),
-    ("g_fan", 0, 1, 3),
+    ("g_pass", 0, 0, 1),
+    ("g_pass", 0, 1, 1),
     ("upd0", 1),
     ("upd1", 1),
     ("upd2", 1),
     ("g_own", 1, 0),
     ("g_own", 1, 1),
+    ("g_fan", 1, 1, 0),
+    ("g_pass", 0, 1, 3),
     ("g_fan", 1, 0, 0),
-    ("g_pass", 0, 1, 1),
-    ("g_last", 0, 1, 0),
-    ("g_pass", 0, 0, 2),
-    ("g_fan", 1, 1, 0),
+    ("g_pass", 0, 0, 3),
+    ("g_last", 0, 0, 1),
+    ("g_near", 1, 0),
     ("g_near", 1, 1),
-    ("g_near", 1, 0),
-    ("g_fan", 1, 0, 2),
+    ("g_fan", 1, 1, 2),
     ("g_fan", 1, 1, 1),
     ("g_fan", 1, 0, 1),
-    ("g_fan", 1, 1, 2),
-    ("g_pass", 0, 1, 2),
+    ("g_fan", 1, 0, 2),
     ("g_fan", 1, 0, 3),
-    ("g_pass", 0, 0, 3),
+    ("g_last", 0, 1, 2),
+    ("g_last", 0, 1, 3),
     ("g_fan", 1, 1, 3),
-    ("g_pass", 0, 1, 3),
-    ("g_pass", 0, 0, 1),
     ("g_pass", 1, 0, 1),
     ("g_pass", 1, 1, 0),
+    ("g_last", 0, 0, 0),
+    ("g_last", 0, 1, 0),
     ("g_pass", 1, 1, 2),
     ("g_pass", 1, 0, 0),
-    ("g_pass", 1, 0, 3),
-    ("g_last", 0, 1, 1),
     ("g_pass", 1, 0, 2),
-    ("g_last", 0, 0, 0),
     ("g_pass", 1, 1, 1),
     ("g_pass", 1, 1, 3),
+    ("g_pass", 1, 0, 3),
+    ("g_last", 1, 0, 1),
+    ("g_last", 1, 1, 0),
+    ("g_last", 0, 1, 1),
+    ("g_last", 1, 0, 0),
+    ("g_last", 0, 0, 3),
     ("g_last", 0, 0, 2),
-    ("g_last", 1, 0, 1),
+    ("g_last", 1, 1, 1),
     ("g_last", 1, 1, 2),
-    ("g_last", 0, 1, 3),
-    ("g_last", 0, 1, 2),
-    ("g_last", 1, 0, 0),
-    ("g_last", 1, 1, 0),
-    ("g_last", 0, 0, 3),
-    ("g_last", 0, 0, 1),
-    ("g_last", 1, 1, 1),
+    ("g_last", 1, 0, 2),
+    ("g_end", 0),
+    ("g_last", 1, 1, 3),
     ("g_last", 1, 0, 3),
-    ("g_last", 1, 0, 2),
-    ("g_last", 1, 1, 3),
     ("g_end", 1),
-    ("g_end", 0),
 )
 
 
@@ -245,68 +266,95 @@
                 mh = 2 * m + h
                 send(source(m, h, da, other), sib.at[mh, da], sib_ss.at[mh, da], sib_rs.at[mh, da], sibling)
 
+    arrived = set()
+
     def have(m, h, da):
-        own_copies[2 * m + h, da].wait()
-        landed(sib.at[2 * m + h, da], sib_rs.at[2 * m + h, da])
-
-    def pair(mh, da, b, lo):
-        rows = pl.ds(lo, QUART)
+        if (m, h, da) not in arrived:
+            arrived.add((m, h, da))
+            own_copies[2 * m + h, da].wait()
+            landed(sib.at[2 * m + h, da], sib_rs.at[2 * m + h, da])
+
+    def ahead(h, k, i):
+        return wrap(pos[h][1] + (2 - i if k == 0 else 3 * (1 - i)))
+
+    def pair(mh, da, b, rows):
         return own[mh, da, b, rows, :].astype(jnp.float32) + sib[mh, da, b, rows, :].astype(jnp.float32)
 
-    def far(m, h):
+    def piece(t, q):
+        n = QUART // SPLIT
+        at = lax.rem(t, SPLIT) * n
+        return (
+            lax.div(t, SPLIT), pl.ds(pl.multiple_of(at, n), n), pl.ds(pl.multiple_of(QUART * q + at, n), n)
+        )
+
+    def far(m, h, k):
         have(m, h, 2)
         mh = 2 * m + h
         for d in range(2):
-            @pl.loop(0, 4)
-            def _(b):
-                s2[mh, d, b] = encode(pair(mh, 2, b, QUART * d), 2 * TOP)
-            send(s2.at[mh, d], r2.at[mh, d], p1_ss.at[mh, d, 0], p1_rs.at[mh, d, 0], along(h, 0, 1 - 2 * d))
-
-    def early(m, h):
+            @pl.loop(0, 2 * SPLIT)
+            def _(t):
+                i, r, rows = piece(t, d)
+                s2[mh, d, k, i, r, :] = encode(pair(mh, 2, ahead(h, k, i), rows), 2 * TOP)
+            send(
+                s2.at[mh, d, k], r2.at[mh, d, k],
+                p1_ss.at[mh, d, 0, k], p1_rs.at[mh, d, 0, k], along(h, 0, 1 - 2 * d),
+            )
+
+    def early(m, h, k):
         mh = 2 * m + h
         for d in range(2):
             have(m, h, 1 + 2 * d)
 
-            @pl.loop(0, 4)
-            def _(b):
-                s1[mh, d, 0, b] = encode(pair(mh, 1 + 2 * d, b, QUART * (1 - d)), 2 * TOP)
-            send(s1.at[mh, d, 0], r1.at[mh, d, 0], p1_ss.at[mh, d, 1], p1_rs.at[mh, d, 1], along(h, 0, 1 - 2 * d))
-
-    def late(m, h):
+            @pl.loop(0, 2 * SPLIT)
+            def _(t):
+                i, r, rows = piece(t, 1 - d)
+                s1[mh, d, 0, k, i, r, :] = encode(pair(mh, 1 + 2 * d, ahead(h, k, i), rows), 2 * TOP)
+            send(
+                s1.at[mh, d, 0, k], r1.at[mh, d, 0, k],
+                p1_ss.at[mh, d, 1, k], p1_rs.at[mh, d, 1, k], along(h, 0, 1 - 2 * d),
+            )
+
+    def late(m, h, k):
         mh = 2 * m + h
         for d in range(2):
-            landed(r2.at[mh, d], p1_rs.at[mh, d, 0])
-
-            @pl.loop(0, 4)
-            def _(b):
-                s1[mh, d, 1, b] = encode(
-                    pair(mh, 1 + 2 * d, b, QUART * d) + decode(r2[mh, d, b], 2 * TOP), 4 * TOP
+            have(m, h, 1 + 2 * d)
+            landed(r2.at[mh, d, k], p1_rs.at[mh, d, 0, k])
+
+            @pl.loop(0, 2 * SPLIT)
+            def _(t):
+                i, r, rows = piece(t, d)
+                s1[mh, d, 1, k, i, r, :] = encode(
+                    pair(mh, 1 + 2 * d, ahead(h, k, i), rows) + decode(r2[mh, d, k, i, r, :], 2 * TOP), 4 * TOP
                 )
-            send(s1.at[mh, d, 1], r1.at[mh, d, 1], p1_ss.at[mh, d, 2], p1_rs.at[mh, d, 2], along(h, 0, 1 - 2 * d))
-
-    def end_early(m, h):
+            send(
+                s1.at[mh, d, 1, k], r1.at[mh, d, 1, k],
+                p1_ss.at[mh, d, 2, k], p1_rs.at[mh, d, 2, k], along(h, 0, 1 - 2 * d),
+            )
+
+    def end_early(m, h, k):
         have(m, h, 0)
         mh = 2 * m + h
         for d in range(2):
-            landed(r1.at[mh, d, 0], p1_rs.at[mh, d, 1])
-
-        @pl.loop(0, 4)
-        def _(b):
+            landed(r1.at[mh, d, 0, k], p1_rs.at[mh, d, 1, k])
+
+        @pl.loop(0, 2 * SPLIT)
+        def _(t):
             for q in range(2):
-                acc[mh, b, pl.ds(QUART * q, QUART), :] = (
-                    pair(mh, 0, b, QUART * q) + decode(r1[mh, 1 - q, 0, b], 2 * TOP)
-                )
-
-    def end_late(m, h):
+                i, r, rows = piece(t, q)
+                b = ahead(h, k, i)
+                acc[mh, b, rows, :] = pair(mh, 0, b, rows) + decode(r1[mh, 1 - q, 0, k, i, r, :], 2 * TOP)
+
+    def end_late(m, h, k):
         mh = 2 * m + h
         for d in range(2):
-            landed(r1.at[mh, d, 1], p1_rs.at[mh, d, 2])
-
-        @pl.loop(0, 4)
-        def _(b):
+            landed(r1.at[mh, d, 1, k], p1_rs.at[mh, d, 2, k])
+
+        @pl.loop(0, 2 * SPLIT)
+        def _(t):
             for q in range(2):
-                rows = pl.ds(QUART * q, QUART)
-                acc[mh, b, rows, :] = acc[mh, b, rows, :] + decode(r1[mh, q, 1, b], 4 * TOP)
+                i, r, rows = piece(t, q)
+                b = ahead(h, k, i)
+                acc[mh, b, rows, :] = acc[mh, b, rows, :] + decode(r1[mh, q, 1, k, i, r, :], 4 * TOP)
 
     def far2(m, h):
         mh, at = 2 * m + h, pos[h][1]
@@ -483,10 +531,10 @@
         scratch_shapes=[
             pltpu.VMEM((4, 4, 4, HALF, width), bf16),
             pltpu.VMEM((4, 4, 4, HALF, width), bf16),
-            pltpu.VMEM((4, 2, 4, QUART, width), WIRE),
-            pltpu.VMEM((4, 2, 4, QUART, width), WIRE),
-            pltpu.VMEM((4, 2, 2, 4, QUART, width), WIRE),
-            pltpu.VMEM((4, 2, 2, 4, QUART, width), WIRE),
+            pltpu.VMEM((4, 2, 2, 2, QUART, width), WIRE),
+            pltpu.VMEM((4, 2, 2, 2, QUART, width), WIRE),
+            pltpu.VMEM((4, 2, 2, 2, 2, QUART, width), WIRE),
+            pltpu.VMEM((4, 2, 2, 2, 2, QUART, width), WIRE),
             pltpu.VMEM((4, 4, HALF, width), f32),
             pltpu.VMEM((4, 2, QUART, width), WIRE),
             pltpu.VMEM((4, 2, QUART, width), WIRE),
@@ -501,7 +549,7 @@
             pltpu.VMEM((2, nz - 1, group, BLK), f32),
             pltpu.VMEM((2, nz, group, BLK), f32),
             dma((2, 2)), dma((4, 4)), dma((4, 4)), dma((4, 4)),
-            dma((4, 2, 3)), dma((4, 2, 3)), dma((4, 2, 3)), dma((4, 2, 3)),
+            dma((4, 2, 3, 2)), dma((4, 2, 3, 2)), dma((4, 2, 3)), dma((4, 2, 3)),
             dma((2, nz - 1)), dma((2,)), dma((2, nz - 1)), dma((2,)),
             dma((4, 4)), dma((4, 4)), dma((4, 4, 4)), dma((4, 4, 4)), dma((4, 16)), dma((2,)),
         ],

time: 90.1 us -> 85.5 us (0.949)
  Pallas kernels: 89.3 us -> 84.8 us
    pallas_call x1, Pallas kernels: 85.1 us -> 80.5 us  [call(): pl.pallas_call(functools.partial(kernel, nz, width), out_shape=(new, new,...]
where the time goes in v5:
time: 85.5 us; the launch traced here: 85.4 us
  Pallas kernels  84.8 us (99%)
    pallas_call x1, Pallas kernels, call(): pl.pallas_call(functools.partial(kernel, nz, width), out_shape=(new, new,...  80.5 us
    pallas_call x1, Pallas kernels, store(): pl.pallas_call(store_kernel, out_shape=tuple((jax.ShapeDtypeStruct(h.shap...  4.25 us

profile of v5, /device:TPU:1, one launch (start us, length us, event | category | flops | bytes accessed | tf_op | source)
XLA Modules:
  0.0 85.4 jit_solution(725707690120938112)
XLA Ops:
  0.6 80.5 %shard_map.93 = (f32[128,640]{1,0:T(8,128)S(1)}, f32[128,640]{1,0:T(8,128)S(1)}, bf16[4,4,2,128,640]{4,3,2,1,0:T(8,128)(2,1)S(1)}, bf16[4,4,2,128,640]{4,3,2,1,0:T(8,128)(2,1)S(1)}) custom-call(bf16[4,4,2,128,640]{4,3,2,1,0:T(8,128)(2,1)} %bitcast.4, bf16[4,4,2,128,640]{4,3,2,1,0:T(8,128)(2,1)} %bitcast.5, f32[128,640]{1,0:T(8,128)} %mom_down.1, ...), custom_call_target="tpu_custom_call" | custom-call | tf_op jit(solution)/shard_map/pallas_call | solution.py:526
  81.2 4.2 %shard_map.94 = (f32[128,640]{1,0:T(8,128)}, f32[128,640]{1,0:T(8,128)}, bf16[4,4,2,128,640]{4,3,2,1,0:T(8,128)(2,1)}, bf16[4,4,2,128,640]{4,3,2,1,0:T(8,128)(2,1)}) custom-call(f32[128,640]{1,0:T(8,128)S(1)} %get-tuple-element.12.refs_0_, f32[128,640]{1,0:T(8,128)S(1)} %get-tuple-element.13.refs_1_, ...), custom_call_target="tpu_custom_call" | custom-call | tf_op jit(solution)/shard_map/pallas_call | solution.py:575

commit v6 on v5

--- a/solution.py
+++ b/solution.py
@@ -218,12 +218,8 @@
             src_ref=src, dst_ref=dst, send_sem=ss, recv_sem=rs, device_id=dev, device_id_type=MESH
         )
 
-    sends = []
-
     def send(src, dst, ss, rs, dev):
-        copy = remote(src, dst, ss, rs, dev)
-        copy.start()
-        sends.append(copy)
+        remote(src, dst, ss, rs, dev).start()
 
     def landed(dst, rs):
         pltpu.make_async_copy(dst, dst, rs).wait()
@@ -264,7 +260,7 @@
         for da in order:
             for h in range(2):
                 mh = 2 * m + h
-                send(source(m, h, da, other), sib.at[mh, da], sib_ss.at[mh, da], sib_rs.at[mh, da], sibling)
+                send(source(m, h, da, other), sib.at[mh, da], sib_ss.at[0], sib_rs.at[mh, da], sibling)
 
     arrived = set()
 
@@ -297,7 +293,7 @@
                 s2[mh, d, k, i, r, :] = encode(pair(mh, 2, ahead(h, k, i), rows), 2 * TOP)
             send(
                 s2.at[mh, d, k], r2.at[mh, d, k],
-                p1_ss.at[mh, d, 0, k], p1_rs.at[mh, d, 0, k], along(h, 0, 1 - 2 * d),
+                p1_ss.at[mh, 0], p1_rs.at[mh, d, 0, k], along(h, 0, 1 - 2 * d),
             )
 
     def early(m, h, k):
@@ -311,7 +307,7 @@
                 s1[mh, d, 0, k, i, r, :] = encode(pair(mh, 1 + 2 * d, ahead(h, k, i), rows), 2 * TOP)
             send(
                 s1.at[mh, d, 0, k], r1.at[mh, d, 0, k],
-                p1_ss.at[mh, d, 1, k], p1_rs.at[mh, d, 1, k], along(h, 0, 1 - 2 * d),
+                p1_ss.at[mh, 1], p1_rs.at[mh, d, 1, k], along(h, 0, 1 - 2 * d),
             )
 
     def late(m, h, k):
@@ -328,7 +324,7 @@
                 )
             send(
                 s1.at[mh, d, 1, k], r1.at[mh, d, 1, k],
-                p1_ss.at[mh, d, 2, k], p1_rs.at[mh, d, 2, k], along(h, 0, 1 - 2 * d),
+                p1_ss.at[mh, 1], p1_rs.at[mh, d, 2, k], along(h, 0, 1 - 2 * d),
             )
 
     def end_early(m, h, k):
@@ -360,14 +356,14 @@
         mh, at = 2 * m + h, pos[h][1]
         for d in range(2):
             t2[mh, d] = encode(acc[mh, wrap(at + 2), pl.ds(QUART * d, QUART), :], 8 * TOP)
-            send(t2.at[mh, d], rr2.at[mh, d], p2_ss.at[mh, d, 0], p2_rs.at[mh, d, 0], along(h, 1, 1 - 2 * d))
+            send(t2.at[mh, d], rr2.at[mh, d], p2_ss.at[mh, 0], p2_rs.at[mh, d, 0], along(h, 1, 1 - 2 * d))
 
     def early2(m, h):
         mh, at = 2 * m + h, pos[h][1]
         for d in range(2):
             near = acc[mh, wrap(at + 1 - 2 * d), pl.ds(QUART * (1 - d), QUART), :]
             t1[mh, d, 0] = encode(near, 8 * TOP)
-            send(t1.at[mh, d, 0], rr1.at[mh, d, 0], p2_ss.at[mh, d, 1], p2_rs.at[mh, d, 1], along(h, 1, 1 - 2 * d))
+            send(t1.at[mh, d, 0], rr1.at[mh, d, 0], p2_ss.at[mh, 1], p2_rs.at[mh, d, 1], along(h, 1, 1 - 2 * d))
 
     def late2(m, h):
         mh = 2 * m + h
@@ -375,7 +371,7 @@
             landed(rr2.at[mh, d], p2_rs.at[mh, d, 0])
             near = acc[mh, wrap(pos[h][1] + 1 - 2 * d), pl.ds(QUART * d, QUART), :]
             t1[mh, d, 1] = encode(near + decode(rr2[mh, d], 8 * TOP), 16 * TOP)
-            send(t1.at[mh, d, 1], rr1.at[mh, d, 1], p2_ss.at[mh, d, 2], p2_rs.at[mh, d, 2], along(h, 1, 1 - 2 * d))
+            send(t1.at[mh, d, 1], rr1.at[mh, d, 1], p2_ss.at[mh, 1], p2_rs.at[mh, d, 2], along(h, 1, 1 - 2 * d))
 
     def end2(m, h):
         if m == 0 and h == 0:
@@ -404,7 +400,7 @@
         gpart[m] = gram.reshape(nz, BLK // nz, BLK)
         for k in range(1, nz):
             to = lax.rem(z + k, nz)
-            send(gpart.at[m, to], gslot.at[m, k - 1], ga_ss.at[m, k - 1], ga_rs.at[m], device(x, y, c, to))
+            send(gpart.at[m, to], gslot.at[m, k - 1], ga_ss.at[m], ga_rs.at[m], device(x, y, c, to))
 
     def gram_sum(m):
         landed(gslot.at[m], ga_rs.at[m])
@@ -414,7 +410,7 @@
         gfull[m, z] = total
         for k in range(1, nz):
             to = lax.rem(z + k, nz)
-            send(gfull.at[m, z], gfull.at[m, z], gb_ss.at[m, k - 1], gb_rs.at[m], device(x, y, c, to))
+            send(gfull.at[m, z], gfull.at[m, z], gb_ss.at[m], gb_rs.at[m], device(x, y, c, to))
 
     def upd0(m):
         landed(gslot.at[m], gb_rs.at[m])
@@ -450,12 +446,12 @@
 
     def hand(m, h, k, a, b):
         ref = block(m, h, a, b)
-        send(ref, ref, as_ss.at[2 * m + h, k], as_rs.at[m], sibling)
+        send(ref, ref, as_ss.at[m], as_rs.at[m], sibling)
 
     def fan(m, h, j, a):
         mh, ref = 2 * m + h, block(m, h, a, pos[h][1])
         for d in range(2):
-            send(ref, ref, ab_ss.at[mh, j, d], ab_rs.at[mh, j, d], along(h, 1, 1 - 2 * d))
+            send(ref, ref, ab_ss.at[mh], ab_rs.at[mh, j, d], along(h, 1, 1 - 2 * d))
 
     def cols(h):
         a = pos[h][0]
@@ -464,7 +460,7 @@
     def g_own(m, h):
         ref = block(m, h, *pos[h])
         for d in range(2):
-            send(ref, ref, aa_ss.at[2 * m + h, d], aa_rs.at[2 * m + h, d], along(h, 0, 1 - 2 * d))
+            send(ref, ref, aa_ss.at[2 * m + h], aa_rs.at[2 * m + h, d], along(h, 0, 1 - 2 * d))
 
     def g_near(m, h):
         mh, b = 2 * m + h, pos[h][1]
@@ -472,7 +468,7 @@
             col = cols(h)[1 + d]
             landed(block(m, h, col, b), aa_rs.at[mh, d])
             part = block(m, h, col, b, QUART * d, QUART)
-            send(part, part, aa_ss.at[mh, 2 + d], aa_rs.at[mh, 2 + d], along(h, 0, 1 - 2 * d))
+            send(part, part, aa_ss.at[mh], aa_rs.at[mh, 2 + d], along(h, 0, 1 - 2 * d))
 
     def g_fan(m, h, j):
         mh, b = 2 * m + h, pos[h][1]
@@ -490,7 +486,7 @@
             row = wrap(b - 1 + 2 * d)
             landed(block(m, h, col, row), ab_rs.at[mh, j, d])
             part = block(m, h, col, row, QUART * d, QUART)
-            send(part, part, ab_ss.at[mh, j, 2 + d], ab_rs.at[mh, j, 2 + d], along(h, 1, 1 - 2 * d))
+            send(part, part, ab_ss.at[mh], ab_rs.at[mh, j, 2 + d], along(h, 1, 1 - 2 * d))
             hand(m, h, 4 + 3 * j + d, col, row)
 
     def g_last(m, h, j):
@@ -511,8 +507,18 @@
     )
     for name, *at in STEPS:
         steps[name](*at)
-    for copy in sends:
-        copy.wait_send()
+    landed(sib, sib_ss.at[0])
+    for mh in range(4):
+        landed(s2.at[mh], p1_ss.at[mh, 0])
+        landed(s1.at[mh], p1_ss.at[mh, 1])
+        landed(t2.at[mh], p2_ss.at[mh, 0])
+        landed(t1.at[mh], p2_ss.at[mh, 1])
+        landed(own.at[0, 0, pl.ds(0, 3)], aa_ss.at[mh])
+        landed(own.at[0, pl.ds(0, 3)], ab_ss.at[mh])
+    for m in range(2):
+        landed(gslot.at[m], ga_ss.at[m])
+        landed(gslot.at[m], gb_ss.at[m])
+        landed(outs[m].at[:, :, c], as_ss.at[m])
 
 
 def call(nz, width, *args):
@@ -548,10 +554,10 @@
             pltpu.VMEM((2, nz, group, BLK), f32),
             pltpu.VMEM((2, nz - 1, group, BLK), f32),
             pltpu.VMEM((2, nz, group, BLK), f32),
-            dma((2, 2)), dma((4, 4)), dma((4, 4)), dma((4, 4)),
-            dma((4, 2, 3, 2)), dma((4, 2, 3, 2)), dma((4, 2, 3)), dma((4, 2, 3)),
-            dma((2, nz - 1)), dma((2,)), dma((2, nz - 1)), dma((2,)),
-            dma((4, 4)), dma((4, 4)), dma((4, 4, 4)), dma((4, 4, 4)), dma((4, 16)), dma((2,)),
+            dma((2, 2)), dma((4, 4)), dma((1,)), dma((4, 4)),
+            dma((4, 2)), dma((4, 2, 3, 2)), dma((4, 2)), dma((4, 2, 3)),
+            dma((2,)), dma((2,)), dma((2,)), dma((2,)),
+            dma((4,)), dma((4, 4)), dma((4,)), dma((4, 4, 4)), dma((2,)), dma((2,)),
         ],
         compiler_params=pltpu.CompilerParams(
             collective_id=0, has_side_effects=True, vmem_limit_bytes=44 * 1024 * 1024

time: 85.5 us -> 83.1 us (0.972)
  Pallas kernels: 84.8 us -> 82.4 us
    pallas_call x1, Pallas kernels: 80.5 us -> 78.1 us  [call(): pl.pallas_call(functools.partial(kernel, nz, width), out_shape=(new, new,...]
where the time goes in v6:
time: 83.1 us; the launch traced here: 83 us
  Pallas kernels  82.4 us (99%)
    pallas_call x1, Pallas kernels, call(): pl.pallas_call(functools.partial(kernel, nz, width), out_shape=(new, new,...  78.1 us
    pallas_call x1, Pallas kernels, store(): pl.pallas_call(store_kernel, out_shape=tuple((jax.ShapeDtypeStruct(h.shap...  4.25 us

profile of v6, /device:TPU:1, one launch (start us, length us, event | category | flops | bytes accessed | tf_op | source)
XLA Modules:
  0.0 83.0 jit_solution(13807239062382449045)
XLA Ops:
  0.6 78.1 %shard_map.93 = (f32[128,640]{1,0:T(8,128)S(1)}, f32[128,640]{1,0:T(8,128)S(1)}, bf16[4,4,2,128,640]{4,3,2,1,0:T(8,128)(2,1)S(1)}, bf16[4,4,2,128,640]{4,3,2,1,0:T(8,128)(2,1)S(1)}) custom-call(bf16[4,4,2,128,640]{4,3,2,1,0:T(8,128)(2,1)} %bitcast.4, bf16[4,4,2,128,640]{4,3,2,1,0:T(8,128)(2,1)} %bitcast.5, f32[128,640]{1,0:T(8,128)} %mom_down.1, ...), custom_call_target="tpu_custom_call" | custom-call | tf_op jit(solution)/shard_map/pallas_call | solution.py:532
  78.8 4.2 %shard_map.94 = (f32[128,640]{1,0:T(8,128)}, f32[128,640]{1,0:T(8,128)}, bf16[4,4,2,128,640]{4,3,2,1,0:T(8,128)(2,1)}, bf16[4,4,2,128,640]{4,3,2,1,0:T(8,128)(2,1)}) custom-call(f32[128,640]{1,0:T(8,128)S(1)} %get-tuple-element.12.refs_0_, f32[128,640]{1,0:T(8,128)S(1)} %get-tuple-element.13.refs_1_, ...), custom_call_target="tpu_custom_call" | custom-call | tf_op jit(solution)/shard_map/pallas_call | solution.py:581

commit v7 on v6

--- a/solution.py
+++ b/solution.py
@@ -49,57 +49,57 @@
 STEPS = (
     ("far", 0, 0, 0),
     ("far", 0, 1, 0),
+    ("far", 0, 1, 1),
     ("far", 0, 0, 1),
-    ("far", 0, 1, 1),
     ("early", 0, 0, 0),
     ("early", 0, 1, 0),
     ("late", 0, 0, 0),
     ("late", 0, 1, 0),
     ("early", 0, 0, 1),
+    ("early", 0, 1, 1),
     ("late", 0, 0, 1),
-    ("early", 0, 1, 1),
+    ("end_early", 0, 0, 0),
     ("late", 0, 1, 1),
-    ("end_early", 0, 0, 0),
+    ("end_early", 0, 1, 0),
     ("end_late", 0, 0, 0),
+    ("end_late", 0, 1, 0),
     ("far2", 0, 0),
-    ("end_early", 0, 1, 0),
-    ("end_late", 0, 1, 0),
     ("far2", 0, 1),
+    ("far", 1, 0, 0),
     ("far", 1, 1, 0),
-    ("far", 1, 0, 0),
+    ("end_early", 0, 1, 1),
     ("end_early", 0, 0, 1),
-    ("end_early", 0, 1, 1),
     ("end_late", 0, 0, 1),
     ("early2", 0, 0),
     ("end_late", 0, 1, 1),
     ("early2", 0, 1),
     ("late2", 0, 0),
     ("late2", 0, 1),
+    ("early", 1, 0, 0),
     ("early", 1, 1, 0),
-    ("far", 1, 0, 1),
-    ("early", 1, 0, 0),
-    ("late", 1, 0, 0),
     ("far", 1, 1, 1),
     ("late", 1, 1, 0),
+    ("far", 1, 0, 1),
+    ("late", 1, 0, 0),
     ("end2", 0, 0),
     ("end2", 0, 1),
     ("gram_send", 0),
     ("early", 1, 1, 1),
     ("early", 1, 0, 1),
     ("late", 1, 1, 1),
+    ("end_early", 1, 1, 0),
+    ("late", 1, 0, 1),
+    ("end_late", 1, 1, 0),
     ("end_early", 1, 0, 0),
-    ("late", 1, 0, 1),
-    ("end_early", 1, 1, 0),
     ("end_late", 1, 0, 0),
+    ("gram_sum", 0),
     ("far2", 1, 0),
-    ("gram_sum", 0),
-    ("end_late", 1, 1, 0),
     ("far2", 1, 1),
     ("end_early", 1, 1, 1),
     ("end_late", 1, 1, 1),
+    ("early2", 1, 1),
     ("end_early", 1, 0, 1),
     ("end_late", 1, 0, 1),
-    ("early2", 1, 1),
     ("early2", 1, 0),
     ("late2", 1, 0),
     ("late2", 1, 1),
@@ -113,22 +113,22 @@
     ("gram_send", 1),
     ("g_fan", 0, 1, 0),
     ("g_fan", 0, 0, 0),
+    ("g_near", 0, 0),
     ("g_near", 0, 1),
-    ("g_near", 0, 0),
+    ("g_fan", 0, 1, 1),
     ("g_fan", 0, 0, 2),
     ("g_fan", 0, 1, 2),
-    ("g_fan", 0, 1, 1),
     ("g_fan", 0, 0, 1),
     ("gram_sum", 1),
+    ("g_fan", 0, 0, 3),
+    ("g_fan", 0, 1, 3),
+    ("g_pass", 0, 0, 2),
+    ("g_pass", 0, 1, 1),
+    ("g_pass", 0, 1, 0),
+    ("g_pass", 0, 0, 0),
+    ("upd0", 1),
     ("g_pass", 0, 1, 2),
-    ("g_pass", 0, 0, 2),
-    ("g_pass", 0, 0, 0),
-    ("g_fan", 0, 1, 3),
-    ("g_pass", 0, 1, 0),
-    ("g_fan", 0, 0, 3),
     ("g_pass", 0, 0, 1),
-    ("g_pass", 0, 1, 1),
-    ("upd0", 1),
     ("upd1", 1),
     ("upd2", 1),
     ("g_own", 1, 0),
@@ -136,8 +136,11 @@
     ("g_fan", 1, 1, 0),
     ("g_pass", 0, 1, 3),
     ("g_fan", 1, 0, 0),
+    ("g_last", 0, 1, 0),
+    ("g_last", 0, 0, 1),
+    ("g_last", 0, 0, 2),
+    ("g_last", 0, 1, 2),
     ("g_pass", 0, 0, 3),
-    ("g_last", 0, 0, 1),
     ("g_near", 1, 0),
     ("g_near", 1, 1),
     ("g_fan", 1, 1, 2),
@@ -145,29 +148,26 @@
     ("g_fan", 1, 0, 1),
     ("g_fan", 1, 0, 2),
     ("g_fan", 1, 0, 3),
-    ("g_last", 0, 1, 2),
+    ("g_fan", 1, 1, 3),
+    ("g_pass", 1, 0, 0),
+    ("g_pass", 1, 1, 2),
+    ("g_pass", 1, 1, 0),
+    ("g_last", 0, 1, 1),
+    ("g_last", 0, 0, 3),
     ("g_last", 0, 1, 3),
-    ("g_fan", 1, 1, 3),
     ("g_pass", 1, 0, 1),
-    ("g_pass", 1, 1, 0),
-    ("g_last", 0, 0, 0),
-    ("g_last", 0, 1, 0),
-    ("g_pass", 1, 1, 2),
-    ("g_pass", 1, 0, 0),
+    ("g_pass", 1, 1, 1),
     ("g_pass", 1, 0, 2),
-    ("g_pass", 1, 1, 1),
     ("g_pass", 1, 1, 3),
     ("g_pass", 1, 0, 3),
+    ("g_last", 0, 0, 0),
     ("g_last", 1, 0, 1),
+    ("g_last", 1, 0, 2),
+    ("g_last", 1, 1, 2),
+    ("g_last", 1, 0, 0),
     ("g_last", 1, 1, 0),
-    ("g_last", 0, 1, 1),
-    ("g_last", 1, 0, 0),
-    ("g_last", 0, 0, 3),
-    ("g_last", 0, 0, 2),
+    ("g_end", 0),
     ("g_last", 1, 1, 1),
-    ("g_last", 1, 1, 2),
-    ("g_last", 1, 0, 2),
-    ("g_end", 0),
     ("g_last", 1, 1, 3),
     ("g_last", 1, 0, 3),
     ("g_end", 1),

time: 83.1 us -> 82.8 us (level)
  no operation moved by 1% of the time
where the time goes in v7:
time: 82.8 us; the launch traced here: 82.7 us
  Pallas kernels  82.1 us (99%)
    pallas_call x1, Pallas kernels, call(): pl.pallas_call(functools.partial(kernel, nz, width), out_shape=(new, new,...  77.8 us
    pallas_call x1, Pallas kernels, store(): pl.pallas_call(store_kernel, out_shape=tuple((jax.ShapeDtypeStruct(h.shap...  4.25 us

profile of v7, /device:TPU:1, one launch (start us, length us, event | category | flops | bytes accessed | tf_op | source)
XLA Modules:
  0.0 82.7 jit_solution(17815321661943079866)
XLA Ops:
  0.6 77.8 %shard_map.93 = (f32[128,640]{1,0:T(8,128)S(1)}, f32[128,640]{1,0:T(8,128)S(1)}, bf16[4,4,2,128,640]{4,3,2,1,0:T(8,128)(2,1)S(1)}, bf16[4,4,2,128,640]{4,3,2,1,0:T(8,128)(2,1)S(1)}) custom-call(bf16[4,4,2,128,640]{4,3,2,1,0:T(8,128)(2,1)} %bitcast.4, bf16[4,4,2,128,640]{4,3,2,1,0:T(8,128)(2,1)} %bitcast.5, f32[128,640]{1,0:T(8,128)} %mom_down.1, ...), custom_call_target="tpu_custom_call" | custom-call | tf_op jit(solution)/shard_map/pallas_call | solution.py:532
  78.5 4.2 %shard_map.94 = (f32[128,640]{1,0:T(8,128)}, f32[128,640]{1,0:T(8,128)}, bf16[4,4,2,128,640]{4,3,2,1,0:T(8,128)(2,1)}, bf16[4,4,2,128,640]{4,3,2,1,0:T(8,128)(2,1)}) custom-call(f32[128,640]{1,0:T(8,128)S(1)} %get-tuple-element.12.refs_0_, f32[128,640]{1,0:T(8,128)S(1)} %get-tuple-element.13.refs_1_, ...), custom_call_target="tpu_custom_call" | custom-call | tf_op jit(solution)/shard_map/pallas_call | solution.py:581
